TPU v7x, 128 devices: a whole 4x4x4 slice. The times are simulated.
128 devices in a mesh: gx: 8 (over y, core), gy: 8 (over z, x_lo), gz: 2 (over x_hi).
Axes of the slice: x: 4 (x_hi: 2, x_lo: 2; x = x_hi * 2 + x_lo), y: 4, z: 4, core: 2. Of those that a mesh axis runs over, the one named last changes fastest.
Arguments:
- residual: float32 [64, 256, 1024], P('gz', 'gx', 'gy'), may hold values from -6 to 6
- scale_field: float32 [64, 256, 1024], P('gz', 'gx', 'gy'), may hold values from 0.3 to 3.3
- kappa_sq: float32 [64, 256, 1024], P('gz', 'gx', 'gy'), may hold values from 0.0002 to 0.005
Outputs:
- preconditioned: float32 [64, 256, 1024], P('gz', 'gx', 'gy')
All inputs are finite; a program needn't handle non-finite values.
Results may differ from a plain program's by a relative error of at most 0.00002.
Values sent between devices are 32-bit elements; how exact they have to be, the bound alone decides.
No kernel may reach another device: no remote copies, remote signals or barrier semaphores. Data moves between devices by JAX's collectives and lax.ppermute only.
A program may use at most 192 MiB of HBM per device.

v0:
```python
import math

import jax
import jax.numpy as jnp
from jax import lax
from jax.experimental import pallas as pl
from jax.experimental.pallas import tpu as pltpu
from jax.sharding import PartitionSpec as P

F32 = jnp.float32
VM = pl.BlockSpec(memory_space=pltpu.VMEM)
HBM = pl.BlockSpec(memory_space=pltpu.HBM)
BF16 = jnp.bfloat16
COARSE_SWEEPS = 11
MICROSECONDS = dict(
    k_face_z=0.2,
    k_load=4.0,
    k_face_x=0.2,
    k_pack_own=1.0,
    k_face_y=0.6,
    k_assemble=1.0,
    k_pack=0.3,
    k_down0=2.0,
    k_coeff=2.0,
    k_down12=3.0,
    k_whole=2.0,
    k_up2=0.5,
    k_up1=1.5,
    k_up0=2.5,
)
A0, B0, U0 = 12, 8, 3
A1, U1 = 4, 8


def run(body, args, outs, scratch=(), out_spec=VM, sems=()):
    words = sum(math.prod(s) for s in (*outs, *scratch)) + sum(a.size for a in args)
    return pl.pallas_call(
        body,
        out_shape=[jax.ShapeDtypeStruct(o, F32) for o in outs],
        in_specs=[VM] * len(args),
        out_specs=[out_spec] * len(outs),
        scratch_shapes=[pltpu.VMEM(s, F32) for s in scratch]
        + [pltpu.SemaphoreType.DMA(n) for n in sems],
        compiler_params=pltpu.CompilerParams(vmem_limit_bytes=6 * words + (6 << 20)),
        cost_estimate=pl.CostEstimate(
            flops=0, transcendentals=0, bytes_accessed=int(3.5e6 * MICROSECONDS[body.__name__])
        ),
    )(*args)


def weights(level):
    wh = 0.25**level
    return wh, 2.0 * (0.25 * wh + 2.0 * wh)


def iota(shape, dim):
    return lax.broadcasted_iota(jnp.int32, shape, dim)


def lanes(v, shift):
    return pltpu.roll(v, shift % v.shape[-1], v.ndim - 1)


def rows(v, shift):
    return pltpu.roll(v, shift % v.shape[-2], v.ndim - 2)


def beside(v):
    return (rows(v, 1) + rows(v, -1)) + (lanes(v, 1) + lanes(v, -1))


def around(above, v, below):
    return 0.25 * (above + below) + beside(v)


def factors(s, k, level):
    wh, full = weights(level)
    diagonal = k + full * (s * s)
    sw = s * (0.8 / jnp.where(diagonal > 0.0, diagonal, 1.0))
    return sw, (wh * s) * sw


def unscale(v, s):
    inside = s > 0.0
    return jnp.where(inside, v / jnp.where(inside, s, 1.0), 0.0)


def dot(a, b):
    b = b.astype(BF16)
    high = a.astype(BF16)
    rest = a - high.astype(F32)
    middle = rest.astype(BF16)
    low = (rest - middle.astype(F32)).astype(BF16)
    terms = [jnp.dot(t, b, preferred_element_type=F32) for t in (high, middle, low)]
    return terms[0] + (terms[1] + terms[2])


def dot3(a, b):
    n, r, c = a.shape
    return dot(a.reshape(n * r, c), b).reshape(n, r, b.shape[1])


def blocks(first, count, size, body, unroll=1):
    def one(b, _):
        z = first + size * b
        body(z, pl.ds(z, size))
        return 0

    lax.fori_loop(0, count // size, one, 0, unroll=unroll)


def pair_sum(v):
    v = v.reshape(v.shape[0] // 2, 2, *v.shape[1:])
    return v[:, 0] + v[:, 1]


def select_matrix(shape, source_of, scale=1.0):
    i, o = iota(shape, 0), iota(shape, 1)
    return jnp.where(source_of(i, o), scale, 0.0).astype(F32)


def k_face_z(g, c, s, zmsg):
    upper = lax.axis_index("gz") == 0
    zmsg[0:3] = g[...]
    zmsg[3:5] = jnp.where(upper, c[1:], c[:2])
    zmsg[5:7] = jnp.where(upper, s[1:], s[:2])


def k_load(f, s, k, g, c, sk1, ps, pk):
    def one(z, at):
        sv, kv = s[at], k[at]
        sw, cv = factors(sv, kv, 0)
        g[at] = sw * f[at]
        c[at] = cv
        ps[pl.ds(z // 2, 2)] = pair_sum(sv)
        pk[pl.ds(z // 2, 2)] = pair_sum(kv)

    blocks(0, 32, 4, one, 2)
    a = ps[:, pl.ds(0, 16, 2), :] + ps[:, pl.ds(1, 16, 2), :]
    b = pk[:, pl.ds(0, 16, 2), :] + pk[:, pl.ds(1, 16, 2), :]
    left = select_matrix((128, 128), lambda i, o: i // 2 == o, 0.125)
    right = select_matrix((128, 128), lambda i, o: i // 2 == o - 64, 0.125)
    sk1[...] = dot3(a, left) + dot3(b, right)


def halo_rows(zr, iz, field, z):
    first, depth = ((0, 3), (3, 2), (5, 2))[field]
    d = z - 35 if z > 34 else 2 - z
    if d >= depth:
        return jnp.zeros(zr.shape[1:], F32)
    row = first + (d if z > 34 else depth - 1 - d)
    return jnp.where(iz == (0 if z > 34 else 1), zr[row], 0.0)


def k_face_x(g, c, s, zr, to_right, to_left):
    iz = lax.axis_index("gz")
    sub = iota((8, 128), 0)

    def put(z, gz, cz, sz):
        a, b, d = gz[24:32], cz[24:32], sz[24:32]
        to_right[z] = jnp.where(sub >= 5, a, jnp.where(sub >= 3, rows(b, -3), rows(d, -5)))
        a, b, d = gz[0:8], cz[0:8], sz[0:8]
        to_left[z] = jnp.where(sub < 3, a, jnp.where(sub < 5, rows(b, 3), rows(d, 5)))

    def one(z, _):
        put(z + 3, g[z], c[z], s[z])
        return 0

    lax.fori_loop(0, 32, one, 0, unroll=4)
    for z in (0, 1, 2, 35, 36, 37):
        put(z, *[halo_rows(zr, iz, n, z) for n in range(3)])


def k_pack_own(g, c, s, *own):
    slot = iota((32, 128), 1)
    for ref, out in zip((g, c, s), own):
        out[...] = jnp.zeros((3, 40, 128), F32)
        for group in range(3):
            total = jnp.zeros((32, 128), F32)
            for j in range(16):
                z = 16 * group + j - 3
                if 0 <= z < 32:
                    total = jnp.where(slot >= 8 * j, lanes(ref[z], 8 * j + 3), total)
                elif z == 32:
                    total = jnp.where(slot >= 8 * j, 0.0, total)
            out[group, :32, :] = total


def side_rows(from_left, from_right, ix, z):
    sub = iota((8, 128), 0)
    lf = jnp.where(ix > 0, from_left[z], 0.0)
    rt = jnp.where(ix < 7, from_right[z], 0.0)
    return (
        jnp.where(sub >= 4, lf, rt),
        jnp.where(sub >= 4, rows(lf, 3), rows(rt, -3)),
        jnp.where(sub >= 4, rows(lf, 5), rows(rt, -5)),
    )


def k_face_y(og, oc, os, zr, from_left, from_right, ag, ac, a_s, to_right, to_left):
    ix, iz = lax.axis_index("gx"), lax.axis_index("gz")
    slot = iota((8, 128), 1)
    wide = iota((32, 128), 1)
    lane = iota((40, 128), 1) % 8
    for group in range(3):
        side = [jnp.zeros((8, 128), F32)] * 3
        mid = [ref[group, :32, :] for ref in (og, oc, os)]
        for j in range(16 if group < 2 else 6):
            z = 16 * group + j
            here = side_rows(from_left, from_right, ix, z)
            for n in range(3):
                side[n] = jnp.where(slot >= 8 * j, lanes(here[n], 8 * j + 3), side[n])
                if z < 3 or z > 34:
                    edge = lanes(halo_rows(zr, iz, n, z), 8 * j + 3)
                    mid[n] = jnp.where(wide // 8 == j, edge, mid[n])
        g, c, s = [jnp.concatenate(parts, axis=0) for parts in zip(mid, side)]
        ag[group] = g
        ac[group] = c
        a_s[group] = s
        to_right[group] = jnp.where(
            lane < 3, g, jnp.where(lane < 5, lanes(c, 2), lanes(s, 4))
        )
        to_left[group] = jnp.where(
            lane >= 6, lanes(c, 3), jnp.where(lane >= 3, g, lanes(s, -2))
        )


def k_assemble(g, c, s, zr, from_left, from_right, gm, cm, sm):
    ix, iz = lax.axis_index("gx"), lax.axis_index("gz")

    def put(z, values):
        for ref, mid, side in zip(
            (gm, cm, sm), values, side_rows(from_left, from_right, ix, z)
        ):
            ref[z] = jnp.concatenate([mid, side], axis=0)

    def one(z, _):
        put(z + 3, (g[z], c[z], s[z]))
        return 0

    lax.fori_loop(0, 32, one, 0, unroll=4)
    for z in (0, 1, 2, 35, 36, 37):
        put(z, [halo_rows(zr, iz, n, z) for n in range(3)])


def near_edges(v):
    lane = iota(v.shape, 2)
    zero = jnp.zeros((1,) + v.shape[1:], F32)
    up, down = lanes(v, 8), lanes(v, -8)
    above = jnp.where(lane < 8, jnp.concatenate([zero, up[:-1]], axis=0), up)
    below = jnp.where(lane >= 120, jnp.concatenate([down[1:], zero], axis=0), down)
    return around(above, v, below)


def joint(v):
    lane = iota((3,) + v.shape[1:], 2)
    return jnp.where(lane % 8 == 4, lanes(v[3:], 2), v[:3])


def near_main(ref, edge, z, n, product=False):
    v = ref[pl.ds(z, n)]
    lane = iota(v.shape, 2)
    e = jnp.stack(
        [
            pltpu.roll(edge[(z + i) // 16], (124 - 8 * ((z + i) % 16)) % 128, 1)
            for i in range(n)
        ]
    )
    if product:
        across = dot3(v, select_matrix((128, 128), lambda i, o: (i == o + 1) | (i == o - 1)))
        across = jnp.where((lane == 0) | (lane == 127), e + across, across)
    else:
        across = jnp.where(lane == 0, e, lanes(v, 1)) + jnp.where(lane == 127, e, lanes(v, -1))
    above, below = ref[pl.ds(z - 1, n)], ref[pl.ds(z + 1, n)]
    return 0.25 * (above + below) + ((rows(v, 1) + rows(v, -1)) + across)


def near(ref, z, n):
    return around(ref[pl.ds(z - 1, n)], ref[pl.ds(z, n)], ref[pl.ds(z + 1, n)])


def k_down0(
    f, gm, cm, sm, og, oc, os, from_left, from_right, gw, cw, sw, q, qw, f1, e, eg, eq
):
    iy = lax.axis_index("gy")
    own = iota((3, 40, 128), 2) % 8 < 3
    lf = jnp.where(iy > 0, from_left[...], 0.0)
    rt = jnp.where(iy < 7, from_right[...], 0.0)

    def windows(ref, right, left):
        mid = ref[...]
        return jnp.concatenate(
            [jnp.where(own, mid, right), jnp.where(own, left, mid)], axis=0
        )

    g = windows(og, rt, lf)
    c = windows(oc, lanes(rt, -3), lanes(lf, -2))
    gw[...] = g
    cw[...] = c
    sw[...] = windows(os, lanes(rt, 2), lanes(lf, -4))
    w = 0.4 * g + c * near_edges(g)
    qw[...] = w
    eg[...] = joint(g)
    eq[...] = joint(w)
    q[0] = jnp.zeros((40, 128), F32)
    q[37] = jnp.zeros((40, 128), F32)

    def relax(z, at):
        q[at] = 0.4 * gm[at] + cm[at] * near_main(gm, eg, z, A0, True)

    blocks(1, 36, A0, relax, U0)

    def residual(z, at):
        v = 0.04 * f[pl.ds(z - 3, B0)] + sm[at, :32, :] * near_main(q, eq, z, B0, True)[:, :32]
        e[pl.ds((z - 3) // 2, B0 // 2)] = pair_sum(v)

    blocks(3, 32, B0, residual, U0)
    a = e[:, pl.ds(0, 16, 2), :] + e[:, pl.ds(1, 16, 2), :]
    lo = select_matrix((128, 128), lambda i, o: i // 2 == o, 0.125)
    hi = select_matrix((128, 128), lambda i, o: i // 2 == o - 64, 0.125)
    f1[...] = dot3(a[:8], lo) + dot3(a[8:], hi)


SLOTS = 5


def k_pack(own, full, to_right, to_left):
    iz = lax.axis_index("gz")
    lane = iota((16, 128), 1) % 64
    n = own.shape[0]
    for group in range(to_right.shape[0]):
        count = min(SLOTS, n - SLOTS * group)
        a, b, kept = None, None, []
        for j in range(count):
            z = SLOTS * group + j
            own_half = iz == (0 if z < n // 2 else 1)
            v = own[z % (n // 2) + jnp.where(own_half, 0, n // 2)]
            kept.append(v)
            last, first = lanes(v, 12 * j - 52), lanes(v, 12 * j) if j else v
            a = last if a is None else jnp.where(lane >= 12 * j, last, a)
            b = first if b is None else jnp.where(lane >= 12 * j, first, b)
        full[SLOTS * group : SLOTS * group + count] = jnp.stack(kept)
        to_right[group] = a
        to_left[group] = b


def joined(own, xl, xr, at, ix):
    lf = jnp.where(ix > 0, xl[at], 0.0)
    rt = jnp.where(ix < 7, xr[at], 0.0)
    sub = iota((rt.shape[0], 8, 128), 1)
    edge = jnp.where(sub < 4, rt[:, 8:16], lf[:, 0:8])
    return jnp.concatenate([own[at], rt[:, 0:8], edge, lf[:, 8:16]], axis=1)


def opened(own, xl, xr, z, n, ix, iy):
    groups = -(-n // SLOTS)
    mid = joined(own, xl, xr, pl.ds(z, 4), ix)
    need = range(z // SLOTS, (z + 3) // SLOTS + 1)
    lf = [joined(own, xl, xr, pl.ds(n + i, 1), ix)[0] for i in need]
    rt = [joined(own, xl, xr, pl.ds(n + groups + i, 1), ix)[0] for i in need]
    lf = [jnp.where(iy > 0, v, 0.0) for v in lf]
    rt = [jnp.where(iy < 7, v, 0.0) for v in rt]
    at = [((z + i) // SLOTS - need[0], (z + i) % SLOTS) for i in range(4)]
    lf = jnp.stack([lanes(lf[i], 116 - 12 * j) for i, j in at])
    rt = jnp.stack([lanes(rt[i], 64 - 12 * j) for i, j in at])
    lane = iota(mid.shape, 2)
    first = jnp.where(lane < 64, mid, jnp.where(lane < 96, rt, lf))
    second = jnp.where(lane >= 64, mid, jnp.where(lane < 32, rt, lf))
    return first, lanes(second, 64)


def halve_x(ref, n, x2):
    x2[:, 14:18, :] = jnp.zeros((n, 4, 128), F32)
    x2[:, 0:14, :] = ref[:, pl.ds(0, 14, 2), :] + ref[:, pl.ds(1, 14, 2), :]
    x2[:, 18:24, :] = ref[:, pl.ds(28, 6, 2), :] + ref[:, pl.ds(29, 6, 2), :]
    return x2[...]


def down_matrix():
    return select_matrix(
        (128, 128),
        lambda i, o: ((i // 2 == o) & (o < 38)) | ((i // 2 == o - 64) & (o >= 122)),
        0.125,
    )


def level3_rows(v, e2):
    half = select_matrix((128, 128), lambda i, o: (i // 2 == o) & (o < 16), 0.125)
    v = v.reshape(8, 2, 24, 128)
    e2[...] = v[:, 0, :8, :] + v[:, 1, :8, :]
    pairs = e2[:, pl.ds(0, 4, 2), :] + e2[:, pl.ds(1, 4, 2), :]
    total = dot(pairs[0], half)
    for j in range(1, 8):
        total = total + lanes(dot(pairs[j], half), 16 * j)
    return total


def k_coeff(own, xl, xr, s1, c1, w1, s2, c2, w2, sk3, ps, pk, x2, e2):
    ix, iy = lax.axis_index("gx"), lax.axis_index("gy")

    for z in range(0, 32, 4):
        at = pl.ds(z, 4)
        s, k = opened(own, xl, xr, z, 32, ix, iy)
        s1[at] = s
        w1[at], c1[at] = factors(s, k, 1)
        ps[pl.ds(z // 2, 2)] = pair_sum(s)
        pk[pl.ds(z // 2, 2)] = pair_sum(k)
    down = down_matrix()
    s = dot3(halve_x(ps, 16, x2), down)
    k = dot3(halve_x(pk, 16, x2), down)
    s2[...] = s
    w2[...], c2[...] = factors(s, k, 2)
    sk3[...] = jnp.concatenate([level3_rows(s, e2), level3_rows(k, e2)], axis=0)


def k_down12(own, xl, xr, s1, c1, w1, s2, c2, w2, sk3, g, q, g2, q2, chunk, f, e, x2, e2):
    ix, iy = lax.axis_index("gx"), lax.axis_index("gy")
    for ref in (g, q):
        ref[0] = jnp.zeros((40, 128), F32)
        ref[33] = jnp.zeros((40, 128), F32)

    for z in range(0, 16, 4):
        for i, v in enumerate(opened(own, xl, xr, z, 16, ix, iy)):
            first = z + 8 * (z // 8) + 8 * i
            f[pl.ds(first, 4)] = v
            g[pl.ds(first + 1, 4)] = w1[pl.ds(first, 4)] * v

    def relax(z, at):
        q[at] = 0.4 * g[at] + c1[pl.ds(z - 1, A1)] * near(g, z, A1)

    blocks(1, 32, A1, relax, U1)
    wh, _ = weights(1)

    def residual(z, at):
        own = pl.ds(z - 1, A1)
        v = 0.04 * f[own] + (wh * s1[own]) * near(q, z, A1)
        e[pl.ds((z - 1) // 2, A1 // 2)] = pair_sum(v)

    blocks(1, 32, A1, residual, U1)
    fv = dot3(halve_x(e, 16, x2), down_matrix())
    gv = w2[...] * fv
    zero = jnp.zeros((1, 24, 128), F32)

    def spread(v):
        w = jnp.concatenate([zero, v, zero], axis=0)
        return around(w[:16], v, w[2:])

    qv = 0.4 * gv + c2[...] * spread(gv)
    wh, _ = weights(2)
    ev = 0.04 * fv + (wh * s2[...]) * spread(qv)
    g2[...] = gv
    q2[...] = qv
    parts = [level3_rows(ev, e2), sk3[:4], sk3[4:]]
    parts = [pltpu.roll(part, 16 * iy, 1) for part in parts]

    def copy(n, _):
        for i in range(3):
            chunk[3 * n + i] = parts[i]
        return 0

    lax.fori_loop(0, 64, copy, 0, unroll=8)


def spread_in(shape, last):
    n, r, _ = shape
    row, col = iota(shape, 1), iota(shape, 2)
    zero = jnp.zeros((1,) + shape[1:], F32)

    def apply(v):
        w = jnp.concatenate([zero, v, zero], axis=0)
        x = jnp.where(row > 0, rows(v, 1), 0.0) + jnp.where(row < r - 1, rows(v, -1), 0.0)
        y = jnp.where(col > 0, lanes(v, 1), 0.0) + jnp.where(col < last, lanes(v, -1), 0.0)
        return 0.25 * (w[:n] + w[2:]) + x + y

    return apply


def k_whole(gathered, u, t3, x4, p3):
    ix, iy = lax.axis_index("gx"), lax.axis_index("gy")
    lane = iota((4, 128), 1) // 16
    for j in range(8):
        for n in range(3):
            for x in range(8):
                v = gathered[x * 24 + n]
                for y in range(1, 8):
                    v = jnp.where(lane == (j + y) % 8, gathered[x * 24 + 3 * y + n], v)
                t3[n, j, 4 * x : 4 * x + 4, :] = lanes(v, -16 * j) if j else v
    f3, s3, k3 = t3[0], t3[1], t3[2]
    near3 = spread_in((8, 32, 128), 127)
    w3, c3 = factors(s3, k3, 3)
    g3 = w3 * f3
    q3 = 0.4 * g3 + c3 * near3(g3)
    e3 = 0.04 * f3 + (weights(3)[0] * s3) * near3(q3)
    half = select_matrix((128, 128), lambda i, o: i // 2 == o, 0.125)
    fields = []
    for v in (e3, s3, k3):
        w = v.reshape(4, 2, 32, 128)
        x4[...] = w[:, 0] + w[:, 1]
        fields.append(dot3(x4[:, pl.ds(0, 16, 2), :] + x4[:, pl.ds(1, 16, 2), :], half))
    f4, s4, k4 = fields
    near4 = spread_in((4, 16, 128), 63)
    w4, c4 = factors(s4, k4, 4)
    g4 = w4 * f4
    v4 = g4
    for _ in range(COARSE_SWEEPS):
        v4 = (0.2 * v4 + g4) + c4 * near4(v4)
    u4 = dot3(unscale(v4, s4), select_matrix((128, 128), lambda i, o: i == o // 2))
    p3[:, pl.ds(0, 16, 2), :] = u4
    p3[:, pl.ds(1, 16, 2), :] = u4
    w = p3[...]
    w = jnp.broadcast_to(w[:, None], (4, 2, 32, 128)).reshape(8, 32, 128)
    v3 = (q3 + 0.8 * g3) + s3 * w
    for _ in range(2):
        v3 = (0.2 * v3 + g3) + c3 * near3(v3)
    pick = select_matrix(
        (128, 128),
        lambda i, o: i == (jnp.where(o < 64, o // 2, 127 - (127 - o) // 2) + 16 * iy) % 128,
    )
    u[...] = pltpu.roll(dot3(v3 / s3, pick), (32 - 4 * ix) % 32, 1)


def k_up2(u3, g2, c2, s2, q2, u, p2):
    p2[:, 14:18, :] = jnp.zeros((8, 4, 128), F32)
    for n in range(2):
        p2[:, pl.ds(n, 7, 2), :] = u3[:, 0:7, :]
        p2[:, pl.ds(18 + n, 3, 2), :] = u3[:, 29:32, :]
    w = p2[...]
    w = jnp.broadcast_to(w[:, None], (8, 2, 24, 128)).reshape(16, 24, 128)
    gv, cv, sv = g2[...], c2[...], s2[...]
    zero = jnp.zeros((1, 24, 128), F32)
    v = (q2[...] + 0.8 * gv) + sv * w
    for _ in range(2):
        w = jnp.concatenate([zero, v, zero], axis=0)
        v = (0.2 * v + gv) + cv * around(w[:16], v, w[2:])
    pick = select_matrix(
        (128, 128),
        lambda i, o: i == jnp.where(o < 96, o // 2, 127 - (127 - o) // 2),
    )
    u[...] = dot3(unscale(v, sv), pick)


def k_up1(u2, g1, c1, s1, q1, u, p1, va, vb):
    for n in range(2):
        p1[:, pl.ds(n, 14, 2), :] = u2[:, 0:14, :]
        p1[:, pl.ds(28 + n, 6, 2), :] = u2[:, 18:24, :]
    for ref in (va, vb, u):
        ref[0] = jnp.zeros((40, 128), F32)
        ref[33] = jnp.zeros((40, 128), F32)

    def start(z, at):
        t = p1[pl.ds((z - 1) // 2, A1 // 2)]
        t = jnp.broadcast_to(t[:, None], (A1 // 2, 2, 40, 128)).reshape(A1, 40, 128)
        va[at] = (q1[at] + 0.8 * g1[at]) + s1[pl.ds(z - 1, A1)] * t

    blocks(1, 32, A1, start, U1)

    def sweep(z, at):
        vb[at] = (0.2 * va[at] + g1[at]) + c1[pl.ds(z - 1, A1)] * near(va, z, A1)

    blocks(1, 32, A1, sweep, U1)

    def last(z, at):
        own = pl.ds(z - 1, A1)
        v = (0.2 * vb[at] + g1[at]) + c1[own] * near(vb, z, A1)
        u[at] = unscale(v, s1[own])

    blocks(1, 32, A1, last, U1)


def k_up0(
    u1, gm, cm, sm, q, gw, cw, sw, qw, out, pm, pw, pv, wa, wb, ea, eb, done, sem
):
    iz = lax.axis_index("gz")

    def source(i, o):
        y = jnp.where(o % 16 < 8, 125 + o % 16, o % 16 - 11)
        return i == jnp.where(o < 128, o // 2, ((y + 256) // 2) % 128)

    u = u1[pl.ds(16 * iz, 18)]
    sub = iota((18, 8, 128), 1)
    u = jnp.concatenate([u[:, :16], jnp.where(sub < 4, u[:, 16:24], u[:, 32:40])], axis=1)
    u = dot3(u, select_matrix((128, 256), source))
    for h, ref in enumerate((pm, pw)):
        w = u[:, :, 128 * h : 128 * h + 128]
        for n in range(2):
            ref[:, pl.ds(n, 18, 2), :] = w[:, 0:18]
            ref[:, pl.ds(36 + n, 2, 2), :] = w[:, 22:24]
    pv[...] = lanes(pw[...], 8)
    slot = iota((40, 128), 1) // 8
    parts = []
    for side in range(2):
        for group in range(3):
            total = None
            for j in range(16):
                ref = pw if j % 2 == side else pv
                part = ref[min(max((16 * group + j - 1) // 2, 0), 17)]
                total = part if total is None else jnp.where(slot >= j, part, total)
            parts.append(total[None])
    g, c = gw[...], cw[...]
    v = (qw[...] + 0.8 * g) + sw[...] * jnp.concatenate(parts, axis=0)
    ea[...] = joint(v)
    eb[...] = joint((0.2 * v + g) + c * near_edges(v))

    def start(z, at):
        t = jnp.stack([pm[(z + i - 1) // 2] for i in range(A0)])
        wa[at] = (q[at] + 0.8 * gm[at]) + sm[at] * t

    blocks(1, 36, A0, start, U0)
    wa[0] = jnp.zeros((40, 128), F32)
    wa[37] = jnp.zeros((40, 128), F32)

    def sweep(z, at):
        wb[at] = (0.2 * wa[at] + gm[at]) + cm[at] * near_main(wa, ea, z, A0, True)

    blocks(1, 36, A0, sweep, U0)

    copies = []
    for b in range(32 // B0):
        z = 3 + b * B0
        at = pl.ds(z, B0)
        n = near_main(wb, eb, z, B0)[:, :32]
        v = (0.2 * wb[at, :32, :] + gm[at, :32, :]) + cm[at, :32, :] * n
        part = pl.ds(z - 3, B0)
        done[part] = v / sm[at, :32, :]
        copies.append(pltpu.make_async_copy(done.at[part], out.at[part], sem.at[b]))
        copies[-1].start()
    for copy in copies:
        copy.wait()


def ring(v, axis, step):
    n = lax.axis_size(axis)
    return lax.ppermute(v, axis, [(i, (i + step) % n) for i in range(n)])


def pair(to_right, to_left, axis):
    return ring(to_right, axis, 1), ring(to_left, axis, -1)


def pack_level1(own):
    n = own.shape[0]
    full, *msg = run(k_pack, (own,), [(n, 16, 128)] + [(-(-n // SLOTS), 16, 128)] * 2)
    return jnp.concatenate([full, *pair(*msg, "gy")], axis=0)


def after(values, *others):
    return lax.optimization_barrier((values, others))[0]


def shards(f, s, k):
    first = jnp.where(lax.axis_index("gz") == 0, 29, 0)
    fz, sz, kz = [lax.dynamic_slice_in_dim(v, first, 3, 0) for v in (f, s, k)]
    sw, c = factors(sz, kz, 0)
    near = (sw * fz, c, jnp.where(kz > 0.0, sz, 0.0))
    zr = ring(run(k_face_z, near, [(7, 32, 128)])[0], "gz", 1)
    g, c, sk1 = run(
        k_load, (f, s, k), [(32, 32, 128)] * 2 + [(16, 16, 128)], [(16, 32, 128)] * 2
    )
    sk1 = after(sk1, zr)
    sk_z = ring(sk1, "gz", 1)
    xs = pair(*run(k_face_x, (g, c, s, zr), [(38, 8, 128)] * 2), "gx")
    small, both = [(3, 40, 128)], [(6, 40, 128)]
    edges = run(k_pack_own, (g, c, s), small * 3)
    *edges, to_right, to_left = run(k_face_y, (*edges, zr, *xs), small * 5)
    ys = pair(to_right, to_left, "gy")
    gm, cm, sm = run(k_assemble, (g, c, s, zr, *xs), [(38, 40, 128)] * 3)
    sk1, sk_z = after((sk1, sk_z), gm)
    sk_y = pack_level1(jnp.concatenate([sk1, sk_z], axis=0))
    gw, cw, sw, q0, qw, f1 = run(
        k_down0,
        (f, gm, cm, sm, *edges, *ys),
        both * 3 + [(38, 40, 128)] + both + [(8, 16, 128)],
        [(16, 32, 128)] + small * 2,
    )
    sk = after(sk_y, f1)
    f1 = jnp.concatenate([f1, ring(f1, "gz", 1)], axis=0)
    s1, c1, w1, s2, c2, w2, sk3 = run(
        k_coeff,
        (sk, *pair(sk, sk, "gx")),
        [(32, 40, 128)] * 3 + [(16, 24, 128)] * 3 + [(8, 128)],
        [(16, 40, 128)] * 2 + [(16, 24, 128), (8, 8, 128)],
    )
    f1 = pack_level1(f1)
    g1, q1, g2, q2, chunk = run(
        k_down12,
        (f1, *pair(f1, f1, "gx"), s1, c1, w1, s2, c2, w2, sk3),
        [(34, 40, 128)] * 2 + [(16, 24, 128)] * 2 + [(192, 4, 128)],
        [(32, 40, 128), (16, 40, 128), (16, 24, 128), (8, 8, 128)],
    )
    gathered = lax.all_to_all(chunk, ("gx", "gy"), 0, 0, tiled=True)
    (u3,) = run(
        k_whole, (gathered,), [(8, 32, 128)], [(3, 8, 32, 128), (4, 32, 128), (4, 32, 128)]
    )
    (u2,) = run(k_up2, (u3, g2, c2, s2, q2), [(16, 24, 128)], [(8, 24, 128)])
    (u1,) = run(
        k_up1, (u2, g1, c1, s1, q1), [(34, 40, 128)], [(16, 40, 128)] + [(34, 40, 128)] * 2
    )
    (out,) = run(
        k_up0,
        (u1, gm, cm, sm, q0, gw, cw, sw, qw),
        [(32, 32, 128)],
        [(18, 40, 128)] * 3 + [(38, 40, 128)] * 2 + small * 2 + [(32, 32, 128)],
        HBM,
        [(32 // B0,)],
    )
    return out


def solution(mesh):
    return jax.shard_map(
        shards,
        mesh=mesh,
        in_specs=(P("gz", "gx", "gy"),) * 3,
        out_specs=P("gz", "gx", "gy"),
        check_vma=False,
    )
```

profile of v0, /device:TPU:1, one launch (start us, length us, event | category | flops | bytes accessed | tf_op | source)
XLA Modules:
  0.0 71.0 jit_solution(11110869322811422800)
XLA Ops:
  0.0 0.9 %compare_select_fusion.1 = (f32[3,32,128]{2,1,0:T(8,128)S(1)}, f32[3,32,128]{2,1,0:T(8,128)S(1)}, f32[3,32,128]{2,1,0:T(8,128)S(1)}) fusion(f32[32,32,128]{2,1,0:T(8,128)} %k.1, s32[]{:T(128)S(6)} %select_n.14, f32[32,32,128]{2,1,0:T(8,128)} %s.7, f32[32,32,128]{2,1,0:T(8,128)} %f.3), kind=kLoop, calls=%fused_computation.7 | loop fusion | flops 135168 | bytes 294916 | tf_op jit(solution)/shard_map/jit(_where)/select_n | solution.py:654
  1.0 3.7 %collective-permute-start = (f32[7,32,128]{2,1,0:T(8,128)S(1)}, f32[7,32,128]{2,1,0:T(8,128)S(1)}, u32[]{:S(2)}, u32[]{:S(2)}) collective-permute-start(f32[7,32,128]{2,1,0:T(8,128)S(1)} %shard_map.38), channel_id=1, source_target_pairs={{0,1},{1,0},{2,3},{3,2},{4,5},{5,4},{6,7},{7,6},{8,9},{9,8},{10,11... | collective-permute-start | bytes 344072 | tf_op jit(solution)/shard_map/ppermute | solution.py:633
  4.6 1.0 %copy-done.1 = f32[32,32,128]{2,1,0:T(8,128)S(1)} copy-done((f32[32,32,128]{2,1,0:T(8,128)S(1)}, f32[32,32,128]{2,1,0:T(8,128)}, u32[]{:S(2)}) %copy-start.1) | copy-done | bytes 524312
  5.7 1.0 %copy-done.3 = f32[32,32,128]{2,1,0:T(8,128)S(1)} copy-done((f32[32,32,128]{2,1,0:T(8,128)S(1)}, f32[32,32,128]{2,1,0:T(8,128)}, u32[]{:S(2)}) %copy-start.3) | copy-done | bytes 524312
  6.7 0.5 shard_map.37
  7.3 2.9 %collective-permute-start.1 = (f32[38,8,128]{2,1,0:T(8,128)S(1)}, f32[38,8,128]{2,1,0:T(8,128)S(1)}, u32[]{:S(2)}, u32[]{:S(2)}) collective-permute-start(f32[38,8,128]{2,1,0:T(8,128)S(1)} %get-tuple-element.51), channel_id=1, source_target_pairs={{0,16},{16,32},{32,48},{48,64},{64,80},{80,96},{96,112},{112,0},{1... | collective-permute-start | bytes 466952 | tf_op jit(solution)/shard_map/ppermute | solution.py:633
  10.2 2.7 %collective-permute-start.10 = (f32[16,16,128]{2,1,0:T(8,128)S(1)}, f32[16,16,128]{2,1,0:T(8,128)S(1)}, u32[]{:S(2)}, u32[]{:S(2)}) collective-permute-start(f32[16,16,128]{2,1,0:T(8,128)S(1)} %get-tuple-element.70), channel_id=1, source_target_pairs={{0,1},{1,0},{2,3},{3,2},{4,5},{5,4},{6,7},{7,6},{8,9},{9,8},{10,11... | collective-permute-start | bytes 393224 | tf_op jit(solution)/shard_map/ppermute | solution.py:633
  13.0 0.5 shard_map.41
  13.5 1.4 %collective-permute-done.2.from_right = f32[38,8,128]{2,1,0:T(8,128)S(1)} collective-permute-done((f32[38,8,128]{2,1,0:T(8,128)S(1)}, f32[38,8,128]{2,1,0:T(8,128)S(1)}, u32[]{:S(2)}, u32[]{:S(2)}) %collective-permute-start.2) | collective-permute-done | bytes 155680 | tf_op jit(solution)/shard_map/ppermute | solution.py:633
  14.9 0.5 shard_map.42
  15.4 1.3 %collective-permute-start.3 = (f32[3,40,128]{2,1,0:T(8,128)S(1)}, f32[3,40,128]{2,1,0:T(8,128)S(1)}, u32[]{:S(2)}, u32[]{:S(2)}) collective-permute-start(f32[3,40,128]{2,1,0:T(8,128)S(1)} %get-tuple-element.62), channel_id=1, source_target_pairs={{0,2},{2,4},{4,6},{6,8},{8,10},{10,12},{12,14},{14,0},{1,3},{3,5},... | collective-permute-start | bytes 184328 | tf_op jit(solution)/shard_map/ppermute | solution.py:633
  16.6 3.6 %collective-permute-start.4 = (f32[3,40,128]{2,1,0:T(8,128)S(1)}, f32[3,40,128]{2,1,0:T(8,128)S(1)}, u32[]{:S(2)}, u32[]{:S(2)}) collective-permute-start(f32[3,40,128]{2,1,0:T(8,128)S(1)} %get-tuple-element.63), channel_id=1, source_target_pairs={{0,14},{2,0},{4,2},{6,4},{8,6},{10,8},{12,10},{14,12},{1,15},{3,1}... | collective-permute-start | bytes 184328 | tf_op jit(solution)/shard_map/ppermute | solution.py:633
  20.2 0.2 shard_map.40
  20.4 0.2 shard_map.45
  20.7 3.6 %collective-permute-start.12 = (f32[7,16,128]{2,1,0:T(8,128)S(1)}, f32[7,16,128]{2,1,0:T(8,128)S(1)}, u32[]{:S(2)}, u32[]{:S(2)}) collective-permute-start(f32[7,16,128]{2,1,0:T(8,128)S(1)} %get-tuple-element.74), channel_id=1, source_target_pairs={{0,14},{2,0},{4,2},{6,4},{8,6},{10,8},{12,10},{14,12},{1,15},{3,1}... | collective-permute-start | bytes 172040 | tf_op jit(solution)/shard_map/ppermute | solution.py:633
  24.3 1.4 %shard_map.43 = (f32[6,40,128]{2,1,0:T(8,128)S(1)}, f32[6,40,128]{2,1,0:T(8,128)S(1)}, f32[6,40,128]{2,1,0:T(8,128)S(1)}, f32[38,40,128]{2,1,0:T(8,128)S(1)}, f3...) custom-call(f32[32,32,128]{2,1,0:T(8,128)S(1)} %copy-done.2, f32[38,40,128]{2,1,0:T(8,128)S(1)} %get-tuple-element.53.gm, ...), custom_call_target="tpu_custom_call" | custom-call | bytes 7000000 | tf_op jit(solution)/shard_map/pallas_call | solution.py:37
  25.8 2.5 %collective-permute-start.5 = (f32[8,16,128]{2,1,0:T(8,128)S(1)}, f32[8,16,128]{2,1,0:T(8,128)S(1)}, u32[]{:S(2)}, u32[]{:S(2)}) collective-permute-start(f32[8,16,128]{2,1,0:T(8,128)S(1)} %get-tuple-element.64), channel_id=1, source_target_pairs={{0,1},{1,0},{2,3},{3,2},{4,5},{5,4},{6,7},{7,6},{8,9},{9,8},{10,11... | collective-permute-start | bytes 196616 | tf_op jit(solution)/shard_map/ppermute | solution.py:633
  28.3 1.2 %collective-permute-start.14 = (f32[46,16,128]{2,1,0:T(8,128)S(1)}, f32[46,16,128]{2,1,0:T(8,128)S(1)}, u32[]{:S(2)}, u32[]{:S(2)}) collective-permute-start(f32[46,16,128]{2,1,0:T(8,128)S(1)} %pad_maximum_fusion.own), channel_id=1, source_target_pairs={{0,112},{16,0},{32,16},{48,32},{64,48},{80,64},{96,80},{112,96},{1... | collective-permute-start | bytes 1130504 | tf_op jit(solution)/shard_map/ppermute | solution.py:633
  29.5 0.6 collective-permute-start.13
  30.1 0.4 collective-permute-done.5
  30.7 3.6 %collective-permute-start.7 = (f32[4,16,128]{2,1,0:T(8,128)S(1)}, f32[4,16,128]{2,1,0:T(8,128)S(1)}, u32[]{:S(2)}, u32[]{:S(2)}) collective-permute-start(f32[4,16,128]{2,1,0:T(8,128)S(1)} %get-tuple-element.67), channel_id=1, source_target_pairs={{0,14},{2,0},{4,2},{6,4},{8,6},{10,8},{12,10},{14,12},{1,15},{3,1}... | collective-permute-start | bytes 98312 | tf_op jit(solution)/shard_map/ppermute | solution.py:633
  34.3 1.3 %collective-permute-done.6 = f32[4,16,128]{2,1,0:T(8,128)S(1)} collective-permute-done((f32[4,16,128]{2,1,0:T(8,128)S(1)}, f32[4,16,128]{2,1,0:T(8,128)S(1)}, u32[]{:S(2)}, u32[]{:S(2)}) %collective-permute-start.6) | collective-permute-done | bytes 32800 | tf_op jit(solution)/shard_map/ppermute | solution.py:633
  35.6 3.2 %collective-permute-start.9 = (f32[24,16,128]{2,1,0:T(8,128)S(1)}, f32[24,16,128]{2,1,0:T(8,128)S(1)}, u32[]{:S(2)}, u32[]{:S(2)}) collective-permute-start(f32[24,16,128]{2,1,0:T(8,128)S(1)} %constant_dynamic-update-slice_fusion.own), channel_id=1, source_target_pairs={{0,112},{16,0},{32,16},{48,32},{64,48},{80,64},{96,80},{112,96},{1... | collective-permute-start | bytes 589832 | tf_op jit(solution)/shard_map/ppermute | solution.py:633
  38.7 0.6 collective-permute-start.8
  39.3 1.6 %shard_map.46 = (f32[32,40,128]{2,1,0:T(8,128)S(1)}, f32[32,40,128]{2,1,0:T(8,128)S(1)}, f32[32,40,128]{2,1,0:T(8,128)S(1)}, f32[16,24,128]{2,1,0:T(8,128)S(1)},...) custom-call(f32[46,16,128]{2,1,0:T(8,128)S(1)} %pad_maximum_fusion.own, ...), custom_call_target="tpu_custom_call" | custom-call | bytes 7000000 | tf_op jit(solution)/shard_map/pallas_call | solution.py:37
  40.9 1.8 %collective-permute-done.9.xr = f32[24,16,128]{2,1,0:T(8,128)S(1)} collective-permute-done((f32[24,16,128]{2,1,0:T(8,128)S(1)}, f32[24,16,128]{2,1,0:T(8,128)S(1)}, u32[]{:S(2)}, u32[]{:S(2)}) %collective-permute-start.9) | collective-permute-done | bytes 196640 | tf_op jit(solution)/shard_map/ppermute | solution.py:633
  42.7 2.4 %shard_map.47 = (f32[34,40,128]{2,1,0:T(8,128)S(1)}, f32[34,40,128]{2,1,0:T(8,128)S(1)}, f32[16,24,128]{2,1,0:T(8,128)S(1)}, f32[16,24,128]{2,1,0:T(8,128)S(1)}, f32[192,4,128]{2,1,0:T(4,128)S(1)}) custom-call(f32[24,16,128]{2,1,0:T(8,128)S(1)} %constant_dynamic-update-slice_fusion.own, f32[24,16,128]{2,1,0:T(8,128)S(1)} %collective-permute-done.8.xl, ...), custom_call_target="tpu_custom_call" | custom-call | bytes 10500000 | tf_op jit(solution)/shard_map/pallas_call | solution.py:37
  45.0 19.7 %all_to_all.5.gathered = f32[192,4,128]{2,1,0:T(4,128)S(1)} all-to-all(f32[192,4,128]{2,1,0:T(4,128)S(1)} %get-tuple-element.83), channel_id=1, replica_groups=mesh['gx'=8,'gy'=8,'gz'=2] {'gx','gy'}, dimensions={0} | all-to-all | bytes 786432 | tf_op jit(solution)/shard_map/all_to_all | solution.py:690
  64.8 2.1 %shard_map.48.u3 = f32[8,32,128]{2,1,0:T(8,128)S(1)} custom-call(f32[192,4,128]{2,1,0:T(4,128)S(1)} %all_to_all.5.gathered), custom_call_target="tpu_custom_call" | custom-call | bytes 7000000 | tf_op jit(solution)/shard_map/pallas_call | solution.py:37
  66.9 0.5 shard_map.49.u2
  67.4 1.0 %shard_map.50.u1 = f32[34,40,128]{2,1,0:T(8,128)S(1)} custom-call(f32[16,24,128]{2,1,0:T(8,128)S(1)} %shard_map.49.u2, f32[34,40,128]{2,1,0:T(8,128)S(1)} %get-tuple-element.86.g1, f32[32,40,128]{2,1,0:T(8,128)S(1)} %get-tuple-element.77.c1, f32[32,40,128]{2,1,0:T(8,128)S(1)} %get-tuple-element.76.s1, f32[34,40,128]{2,1,0:T(8,128)S(1)} %get-tuple-element.87.q1), custom_call_target="tpu_custom_call" | custom-call | bytes 5250000 | tf_op jit(solution)/shard_map/pallas_call | solution.py:37
  68.4 2.4 %shard_map.51 = f32[32,32,128]{2,1,0:T(8,128)} custom-call(f32[34,40,128]{2,1,0:T(8,128)S(1)} %shard_map.50.u1, f32[38,40,128]{2,1,0:T(8,128)S(1)} %get-tuple-element.53.gm, f32[38,40,128]{2,1,0:T(8,128)S(1)} %get-tuple-element.54.cm, f32[38,40,128]{2,1,0:T(8,128)S(1)} %get-tuple-element.55.sm, f32[38,40,128]{2,1,0:T(8,128)S(1)} %get-tuple-element.88.q, ...), custom_call_target="tpu_custom_call" | custom-call | bytes 8750000 | tf_op jit(solution)/shard_map/pallas_call | solution.py:37
  (29 shorter events, 0.5 us)
Async XLA Ops:
  0.0 4.6 %copy-start = (f32[32,32,128]{2,1,0:T(8,128)S(1)}, f32[32,32,128]{2,1,0:T(8,128)}, u32[]{:S(2)}) copy-start(f32[32,32,128]{2,1,0:T(8,128)} %s.7) | copy-start | bytes 1572868
  1.0 6.2 %collective-permute-start = (f32[7,32,128]{2,1,0:T(8,128)S(1)}, f32[7,32,128]{2,1,0:T(8,128)S(1)}, u32[]{:S(2)}, u32[]{:S(2)}) collective-permute-start(f32[7,32,128]{2,1,0:T(8,128)S(1)} %shard_map.38), channel_id=1, source_target_pairs={{0,1},{1,0},{2,3},{3,2},{4,5},{5,4},{6,7},{7,6},{8,9},{9,8},{10,11... | collective-permute-start | bytes 344072 | tf_op jit(solution)/shard_map/ppermute | solution.py:633
  4.6 1.0 %copy-start.1 = (f32[32,32,128]{2,1,0:T(8,128)S(1)}, f32[32,32,128]{2,1,0:T(8,128)}, u32[]{:S(2)}) copy-start(f32[32,32,128]{2,1,0:T(8,128)} %f.3) | copy-start | bytes 1572868
  5.7 1.0 %copy-start.3 = (f32[32,32,128]{2,1,0:T(8,128)S(1)}, f32[32,32,128]{2,1,0:T(8,128)}, u32[]{:S(2)}) copy-start(f32[32,32,128]{2,1,0:T(8,128)} %k.1) | copy-start | bytes 1572868
  7.3 6.1 %collective-permute-start.1 = (f32[38,8,128]{2,1,0:T(8,128)S(1)}, f32[38,8,128]{2,1,0:T(8,128)S(1)}, u32[]{:S(2)}, u32[]{:S(2)}) collective-permute-start(f32[38,8,128]{2,1,0:T(8,128)S(1)} %get-tuple-element.51), channel_id=1, source_target_pairs={{0,16},{16,32},{32,48},{48,64},{64,80},{80,96},{96,112},{112,0},{1... | collective-permute-start | bytes 466952 | tf_op jit(solution)/shard_map/ppermute | solution.py:633
  10.2 4.7 %collective-permute-start.2 = (f32[38,8,128]{2,1,0:T(8,128)S(1)}, f32[38,8,128]{2,1,0:T(8,128)S(1)}, u32[]{:S(2)}, u32[]{:S(2)}) collective-permute-start(f32[38,8,128]{2,1,0:T(8,128)S(1)} %get-tuple-element.52), channel_id=1, source_target_pairs={{0,112},{16,0},{32,16},{48,32},{64,48},{80,64},{96,80},{112,96},{1... | collective-permute-start | bytes 466952 | tf_op jit(solution)/shard_map/ppermute | solution.py:633
  10.2 10.2 %collective-permute-start.10 = (f32[16,16,128]{2,1,0:T(8,128)S(1)}, f32[16,16,128]{2,1,0:T(8,128)S(1)}, u32[]{:S(2)}, u32[]{:S(2)}) collective-permute-start(f32[16,16,128]{2,1,0:T(8,128)S(1)} %get-tuple-element.70), channel_id=1, source_target_pairs={{0,1},{1,0},{2,3},{3,2},{4,5},{5,4},{6,7},{7,6},{8,9},{9,8},{10,11... | collective-permute-start | bytes 393224 | tf_op jit(solution)/shard_map/ppermute | solution.py:633
  15.4 8.9 %collective-permute-start.3 = (f32[3,40,128]{2,1,0:T(8,128)S(1)}, f32[3,40,128]{2,1,0:T(8,128)S(1)}, u32[]{:S(2)}, u32[]{:S(2)}) collective-permute-start(f32[3,40,128]{2,1,0:T(8,128)S(1)} %get-tuple-element.62), channel_id=1, source_target_pairs={{0,2},{2,4},{4,6},{6,8},{8,10},{10,12},{12,14},{14,0},{1,3},{3,5},... | collective-permute-start | bytes 184328 | tf_op jit(solution)/shard_map/ppermute | solution.py:633
  16.6 7.6 %collective-permute-start.4 = (f32[3,40,128]{2,1,0:T(8,128)S(1)}, f32[3,40,128]{2,1,0:T(8,128)S(1)}, u32[]{:S(2)}, u32[]{:S(2)}) collective-permute-start(f32[3,40,128]{2,1,0:T(8,128)S(1)} %get-tuple-element.63), channel_id=1, source_target_pairs={{0,14},{2,0},{4,2},{6,4},{8,6},{10,8},{12,10},{14,12},{1,15},{3,1}... | collective-permute-start | bytes 184328 | tf_op jit(solution)/shard_map/ppermute | solution.py:633
  20.4 3.9 %copy-start.2 = (f32[32,32,128]{2,1,0:T(8,128)S(1)}, f32[32,32,128]{2,1,0:T(8,128)}, u32[]{:S(2)}) copy-start(f32[32,32,128]{2,1,0:T(8,128)} %f.3) | copy-start | bytes 1572868
  20.6 7.6 %collective-permute-start.11 = (f32[7,16,128]{2,1,0:T(8,128)S(1)}, f32[7,16,128]{2,1,0:T(8,128)S(1)}, u32[]{:S(2)}, u32[]{:S(2)}) collective-permute-start(f32[7,16,128]{2,1,0:T(8,128)S(1)} %get-tuple-element.73), channel_id=1, source_target_pairs={{0,2},{2,4},{4,6},{6,8},{8,10},{10,12},{12,14},{14,0},{1,3},{3,5},... | collective-permute-start | bytes 172040 | tf_op jit(solution)/shard_map/ppermute | solution.py:633
  20.7 7.6 %collective-permute-start.12 = (f32[7,16,128]{2,1,0:T(8,128)S(1)}, f32[7,16,128]{2,1,0:T(8,128)S(1)}, u32[]{:S(2)}, u32[]{:S(2)}) collective-permute-start(f32[7,16,128]{2,1,0:T(8,128)S(1)} %get-tuple-element.74), channel_id=1, source_target_pairs={{0,14},{2,0},{4,2},{6,4},{8,6},{10,8},{12,10},{14,12},{1,15},{3,1}... | collective-permute-start | bytes 172040 | tf_op jit(solution)/shard_map/ppermute | solution.py:633
  25.8 4.7 %collective-permute-start.5 = (f32[8,16,128]{2,1,0:T(8,128)S(1)}, f32[8,16,128]{2,1,0:T(8,128)S(1)}, u32[]{:S(2)}, u32[]{:S(2)}) collective-permute-start(f32[8,16,128]{2,1,0:T(8,128)S(1)} %get-tuple-element.64), channel_id=1, source_target_pairs={{0,1},{1,0},{2,3},{3,2},{4,5},{5,4},{6,7},{7,6},{8,9},{9,8},{10,11... | collective-permute-start | bytes 196616 | tf_op jit(solution)/shard_map/ppermute | solution.py:633
  28.3 11.0 %collective-permute-start.14 = (f32[46,16,128]{2,1,0:T(8,128)S(1)}, f32[46,16,128]{2,1,0:T(8,128)S(1)}, u32[]{:S(2)}, u32[]{:S(2)}) collective-permute-start(f32[46,16,128]{2,1,0:T(8,128)S(1)} %pad_maximum_fusion.own), channel_id=1, source_target_pairs={{0,112},{16,0},{32,16},{48,32},{64,48},{80,64},{96,80},{112,96},{1... | collective-permute-start | bytes 1130504 | tf_op jit(solution)/shard_map/ppermute | solution.py:633
  29.5 9.8 %collective-permute-start.13 = (f32[46,16,128]{2,1,0:T(8,128)S(1)}, f32[46,16,128]{2,1,0:T(8,128)S(1)}, u32[]{:S(2)}, u32[]{:S(2)}) collective-permute-start(f32[46,16,128]{2,1,0:T(8,128)S(1)} %pad_maximum_fusion.own), channel_id=1, source_target_pairs={{0,16},{16,32},{32,48},{48,64},{64,80},{80,96},{96,112},{112,0},{1... | collective-permute-start | bytes 1130504 | tf_op jit(solution)/shard_map/ppermute | solution.py:633
  30.6 4.9 %collective-permute-start.6 = (f32[4,16,128]{2,1,0:T(8,128)S(1)}, f32[4,16,128]{2,1,0:T(8,128)S(1)}, u32[]{:S(2)}, u32[]{:S(2)}) collective-permute-start(f32[4,16,128]{2,1,0:T(8,128)S(1)} %get-tuple-element.66), channel_id=1, source_target_pairs={{0,2},{2,4},{4,6},{6,8},{8,10},{10,12},{12,14},{14,0},{1,3},{3,5},... | collective-permute-start | bytes 98312 | tf_op jit(solution)/shard_map/ppermute | solution.py:633
  30.7 4.9 %collective-permute-start.7 = (f32[4,16,128]{2,1,0:T(8,128)S(1)}, f32[4,16,128]{2,1,0:T(8,128)S(1)}, u32[]{:S(2)}, u32[]{:S(2)}) collective-permute-start(f32[4,16,128]{2,1,0:T(8,128)S(1)} %get-tuple-element.67), channel_id=1, source_target_pairs={{0,14},{2,0},{4,2},{6,4},{8,6},{10,8},{12,10},{14,12},{1,15},{3,1}... | collective-permute-start | bytes 98312 | tf_op jit(solution)/shard_map/ppermute | solution.py:633
  35.6 7.1 %collective-permute-start.9 = (f32[24,16,128]{2,1,0:T(8,128)S(1)}, f32[24,16,128]{2,1,0:T(8,128)S(1)}, u32[]{:S(2)}, u32[]{:S(2)}) collective-permute-start(f32[24,16,128]{2,1,0:T(8,128)S(1)} %constant_dynamic-update-slice_fusion.own), channel_id=1, source_target_pairs={{0,112},{16,0},{32,16},{48,32},{64,48},{80,64},{96,80},{112,96},{1... | collective-permute-start | bytes 589832 | tf_op jit(solution)/shard_map/ppermute | solution.py:633
  38.7 3.9 %collective-permute-start.8 = (f32[24,16,128]{2,1,0:T(8,128)S(1)}, f32[24,16,128]{2,1,0:T(8,128)S(1)}, u32[]{:S(2)}, u32[]{:S(2)}) collective-permute-start(f32[24,16,128]{2,1,0:T(8,128)S(1)} %constant_dynamic-update-slice_fusion.own), channel_id=1, source_target_pairs={{0,16},{16,32},{32,48},{48,64},{64,80},{80,96},{96,112},{112,0},{1... | collective-permute-start | bytes 589832 | tf_op jit(solution)/shard_map/ppermute | solution.py:633
where the time goes:
time: 71.2 us; the launch traced here: 71 us
  starting transfers between devices  29.5 us (41%)
  blocking collectives  19.7 us (28%)
  Pallas kernels  13.5 us (19%)
  waiting for transfers between devices  4.87 us (7%)
  local copies, waits for them, and re-layouts  2.11 us (3%)
  other arithmetic  0.98 us (1%)
    ppermute x15, starting transfers between devices, ring(): return lax.ppermute(v, axis, [(i, (i + step) % n) for i in range(n)])  29.5 us
    all_to_all x1, blocking collectives, shards(): gathered = lax.all_to_all(chunk, ('gx', 'gy'), 0, 0, tiled=True)  19.7 us
    pallas_call x15, Pallas kernels, run(): pl.pallas_call(body, out_shape=[jax.ShapeDtypeStruct(o, F32) for o in out...  13.5 us
    ppermute x15, waiting for transfers between devices, ring(): return lax.ppermute(v, axis, [(i, (i + step) % n) for i in range(n)])  4.87 us
    unnamed x10, local copies, waits for them, and re-layouts  2.11 us
  transfers between devices with their start and end apart: 15, of which 4 were waited for; matrix products, arithmetic and copies ran while one was open for 0% of the time, Pallas kernels for 7%

commit v1 on v0

--- a/solution.py
+++ b/solution.py
@@ -171,19 +171,17 @@
         put(z, *[halo_rows(zr, iz, n, z) for n in range(3)])
 
 
-def k_pack_own(g, c, s, *own):
+def k_pack_own(g, c, s, zr, *own):
+    iz = lax.axis_index("gz")
     slot = iota((32, 128), 1)
-    for ref, out in zip((g, c, s), own):
-        out[...] = jnp.zeros((3, 40, 128), F32)
+    for n, (ref, out) in enumerate(zip((g, c, s), own)):
         for group in range(3):
             total = jnp.zeros((32, 128), F32)
-            for j in range(16):
-                z = 16 * group + j - 3
-                if 0 <= z < 32:
-                    total = jnp.where(slot >= 8 * j, lanes(ref[z], 8 * j + 3), total)
-                elif z == 32:
-                    total = jnp.where(slot >= 8 * j, 0.0, total)
-            out[group, :32, :] = total
+            for j in range(16 if group < 2 else 6):
+                z = 16 * group + j
+                here = ref[z - 3] if 3 <= z < 35 else halo_rows(zr, iz, n, z)
+                total = jnp.where(slot >= 8 * j, lanes(here, 8 * j + 3), total)
+            out[group] = total
 
 
 def side_rows(from_left, from_right, ix, z):
@@ -197,22 +195,17 @@
     )
 
 
-def k_face_y(og, oc, os, zr, from_left, from_right, ag, ac, a_s, to_right, to_left):
-    ix, iz = lax.axis_index("gx"), lax.axis_index("gz")
+def k_face_y(og, oc, os, from_left, from_right, ag, ac, a_s, to_right, to_left):
+    ix = lax.axis_index("gx")
     slot = iota((8, 128), 1)
-    wide = iota((32, 128), 1)
     lane = iota((40, 128), 1) % 8
     for group in range(3):
         side = [jnp.zeros((8, 128), F32)] * 3
-        mid = [ref[group, :32, :] for ref in (og, oc, os)]
+        mid = [ref[group] for ref in (og, oc, os)]
         for j in range(16 if group < 2 else 6):
-            z = 16 * group + j
-            here = side_rows(from_left, from_right, ix, z)
+            here = side_rows(from_left, from_right, ix, 16 * group + j)
             for n in range(3):
                 side[n] = jnp.where(slot >= 8 * j, lanes(here[n], 8 * j + 3), side[n])
-                if z < 3 or z > 34:
-                    edge = lanes(halo_rows(zr, iz, n, z), 8 * j + 3)
-                    mid[n] = jnp.where(wide // 8 == j, edge, mid[n])
         g, c, s = [jnp.concatenate(parts, axis=0) for parts in zip(mid, side)]
         ag[group] = g
         ac[group] = c
@@ -384,18 +377,19 @@
     )
 
 
-def level3_rows(v, e2):
+def level3_rows(v, e2, rows2):
     half = select_matrix((128, 128), lambda i, o: (i // 2 == o) & (o < 16), 0.125)
-    v = v.reshape(8, 2, 24, 128)
-    e2[...] = v[:, 0, :8, :] + v[:, 1, :8, :]
-    pairs = e2[:, pl.ds(0, 4, 2), :] + e2[:, pl.ds(1, 4, 2), :]
-    total = dot(pairs[0], half)
+    e2[...] = pair_sum(v)[:, :8, :]
+    for j in range(8):
+        rows2[4 * j : 4 * j + 4] = e2[j, pl.ds(0, 4, 2), :] + e2[j, pl.ds(1, 4, 2), :]
+    pieces = dot(rows2[...], half)
+    total = pieces[0:4]
     for j in range(1, 8):
-        total = total + lanes(dot(pairs[j], half), 16 * j)
+        total = total + lanes(pieces[4 * j : 4 * j + 4], 16 * j)
     return total
 
 
-def k_coeff(own, xl, xr, s1, c1, w1, s2, c2, w2, sk3, ps, pk, x2, e2):
+def k_coeff(own, xl, xr, s1, c1, w1, s2, c2, w2, sk3, ps, pk, x2, e2, r2):
     ix, iy = lax.axis_index("gx"), lax.axis_index("gy")
 
     for z in range(0, 32, 4):
@@ -410,10 +404,10 @@
     k = dot3(halve_x(pk, 16, x2), down)
     s2[...] = s
     w2[...], c2[...] = factors(s, k, 2)
-    sk3[...] = jnp.concatenate([level3_rows(s, e2), level3_rows(k, e2)], axis=0)
-
-
-def k_down12(own, xl, xr, s1, c1, w1, s2, c2, w2, sk3, g, q, g2, q2, chunk, f, e, x2, e2):
+    sk3[...] = jnp.concatenate([level3_rows(s, e2, r2), level3_rows(k, e2, r2)], axis=0)
+
+
+def k_down12(own, xl, xr, s1, c1, w1, s2, c2, w2, sk3, g, q, g2, q2, chunk, f, e, x2, e2, r2):
     ix, iy = lax.axis_index("gx"), lax.axis_index("gy")
     for ref in (g, q):
         ref[0] = jnp.zeros((40, 128), F32)
@@ -450,7 +444,7 @@
     ev = 0.04 * fv + (wh * s2[...]) * spread(qv)
     g2[...] = gv
     q2[...] = qv
-    parts = [level3_rows(ev, e2), sk3[:4], sk3[4:]]
+    parts = [level3_rows(ev, e2, r2), sk3[:4], sk3[4:]]
     parts = [pltpu.roll(part, 16 * iy, 1) for part in parts]
 
     def copy(n, _):
@@ -498,12 +492,23 @@
         x4[...] = w[:, 0] + w[:, 1]
         fields.append(dot3(x4[:, pl.ds(0, 16, 2), :] + x4[:, pl.ds(1, 16, 2), :], half))
     f4, s4, k4 = fields
-    near4 = spread_in((4, 16, 128), 63)
+    zero4, row4 = jnp.zeros((1, 16, 128), F32), iota((4, 16, 128), 1)
+
+    def near4(v, before, after):
+        w = jnp.concatenate([zero4, v, zero4], axis=0)
+        x = jnp.where(row4 > 0, rows(v, 1), 0.0) + jnp.where(row4 < 15, rows(v, -1), 0.0)
+        return (0.25 * (w[:4] + w[2:]) + x) + (before + after)
+
     w4, c4 = factors(s4, k4, 4)
     g4 = w4 * f4
-    v4 = g4
-    for _ in range(COARSE_SWEEPS):
-        v4 = (0.2 * v4 + g4) + c4 * near4(v4)
+    v4 = (0.2 * g4 + g4) + c4 * near4(g4, lanes(g4, 1), lanes(g4, -1))
+    g4m, g4p, c4m, c4p = lanes(g4, 1), lanes(g4, -1), lanes(c4, 1), lanes(c4, -1)
+    for _ in range(COARSE_SWEEPS // 2):
+        vm, vp = lanes(v4, 1), lanes(v4, -1)
+        am = (0.2 * vm + g4m) + c4m * near4(vm, lanes(v4, 2), v4)
+        ap = (0.2 * vp + g4p) + c4p * near4(vp, v4, lanes(v4, -2))
+        a = (0.2 * v4 + g4) + c4 * near4(v4, vm, vp)
+        v4 = (0.2 * a + g4) + c4 * near4(a, am, ap)
     u4 = dot3(unscale(v4, s4), select_matrix((128, 128), lambda i, o: i == o // 2))
     p3[:, pl.ds(0, 16, 2), :] = u4
     p3[:, pl.ds(1, 16, 2), :] = u4
@@ -660,8 +665,8 @@
     sk_z = ring(sk1, "gz", 1)
     xs = pair(*run(k_face_x, (g, c, s, zr), [(38, 8, 128)] * 2), "gx")
     small, both = [(3, 40, 128)], [(6, 40, 128)]
-    edges = run(k_pack_own, (g, c, s), small * 3)
-    *edges, to_right, to_left = run(k_face_y, (*edges, zr, *xs), small * 5)
+    edges = run(k_pack_own, (g, c, s, zr), [(3, 32, 128)] * 3)
+    *edges, to_right, to_left = run(k_face_y, (*edges, *xs), small * 5)
     ys = pair(to_right, to_left, "gy")
     gm, cm, sm = run(k_assemble, (g, c, s, zr, *xs), [(38, 40, 128)] * 3)
     sk1, sk_z = after((sk1, sk_z), gm)
@@ -678,14 +683,14 @@
         k_coeff,
         (sk, *pair(sk, sk, "gx")),
         [(32, 40, 128)] * 3 + [(16, 24, 128)] * 3 + [(8, 128)],
-        [(16, 40, 128)] * 2 + [(16, 24, 128), (8, 8, 128)],
+        [(16, 40, 128)] * 2 + [(16, 24, 128), (8, 8, 128), (32, 128)],
     )
     f1 = pack_level1(f1)
     g1, q1, g2, q2, chunk = run(
         k_down12,
         (f1, *pair(f1, f1, "gx"), s1, c1, w1, s2, c2, w2, sk3),
         [(34, 40, 128)] * 2 + [(16, 24, 128)] * 2 + [(192, 4, 128)],
-        [(32, 40, 128), (16, 40, 128), (16, 24, 128), (8, 8, 128)],
+        [(32, 40, 128), (16, 40, 128), (16, 24, 128), (8, 8, 128), (32, 128)],
     )
     gathered = lax.all_to_all(chunk, ("gx", "gy"), 0, 0, tiled=True)
     (u3,) = run(

time: 71.2 us -> 70.6 us (level)
  Pallas kernels: 13.5 us -> 12.7 us
    pallas_call x15, Pallas kernels: 13.5 us -> 12.7 us  [run(): pl.pallas_call(body, out_shape=[jax.ShapeDtypeStruct(o, F32) for o in out...]
where the time goes in v1:
time: 70.6 us; the launch traced here: 70.4 us
  starting transfers between devices  29.5 us (42%)
  blocking collectives  19.7 us (28%)
  Pallas kernels  12.7 us (18%)
  waiting for transfers between devices  5.02 us (7%)
  local copies, waits for them, and re-layouts  2.11 us (3%)
  other arithmetic  0.98 us (1%)
    ppermute x15, starting transfers between devices, ring(): return lax.ppermute(v, axis, [(i, (i + step) % n) for i in range(n)])  29.5 us
    all_to_all x1, blocking collectives, shards(): gathered = lax.all_to_all(chunk, ('gx', 'gy'), 0, 0, tiled=True)  19.7 us
    pallas_call x15, Pallas kernels, run(): pl.pallas_call(body, out_shape=[jax.ShapeDtypeStruct(o, F32) for o in out...  12.7 us
    ppermute x15, waiting for transfers between devices, ring(): return lax.ppermute(v, axis, [(i, (i + step) % n) for i in range(n)])  5.02 us
    unnamed x10, local copies, waits for them, and re-layouts  2.11 us
  transfers between devices with their start and end apart: 15, of which 4 were waited for; matrix products, arithmetic and copies ran while one was open for 0% of the time, Pallas kernels for 7%

profile of v1, /device:TPU:1, one launch (start us, length us, event | category | flops | bytes accessed | tf_op | source)
XLA Modules:
  0.0 70.4 jit_solution(9844156531409807061)
XLA Ops:
  0.0 0.9 %compare_select_fusion.1 = (f32[3,32,128]{2,1,0:T(8,128)S(1)}, f32[3,32,128]{2,1,0:T(8,128)S(1)}, f32[3,32,128]{2,1,0:T(8,128)S(1)}) fusion(f32[32,32,128]{2,1,0:T(8,128)} %k.1, s32[]{:T(128)S(6)} %select_n.14, f32[32,32,128]{2,1,0:T(8,128)} %s.7, f32[32,32,128]{2,1,0:T(8,128)} %f.3), kind=kLoop, calls=%fused_computation.7 | loop fusion | flops 135168 | bytes 294916 | tf_op jit(solution)/shard_map/jit(_where)/select_n | solution.py:659
  1.0 3.7 %collective-permute-start = (f32[7,32,128]{2,1,0:T(8,128)S(1)}, f32[7,32,128]{2,1,0:T(8,128)S(1)}, u32[]{:S(2)}, u32[]{:S(2)}) collective-permute-start(f32[7,32,128]{2,1,0:T(8,128)S(1)} %shard_map.38), channel_id=1, source_target_pairs={{0,1},{1,0},{2,3},{3,2},{4,5},{5,4},{6,7},{7,6},{8,9},{9,8},{10,11... | collective-permute-start | bytes 344072 | tf_op jit(solution)/shard_map/ppermute | solution.py:638
  4.6 1.0 %copy-done.1 = f32[32,32,128]{2,1,0:T(8,128)S(1)} copy-done((f32[32,32,128]{2,1,0:T(8,128)S(1)}, f32[32,32,128]{2,1,0:T(8,128)}, u32[]{:S(2)}) %copy-start.1) | copy-done | bytes 524312
  5.7 1.0 %copy-done.3 = f32[32,32,128]{2,1,0:T(8,128)S(1)} copy-done((f32[32,32,128]{2,1,0:T(8,128)S(1)}, f32[32,32,128]{2,1,0:T(8,128)}, u32[]{:S(2)}) %copy-start.3) | copy-done | bytes 524312
  6.7 0.5 shard_map.37
  7.3 2.9 %collective-permute-start.1 = (f32[38,8,128]{2,1,0:T(8,128)S(1)}, f32[38,8,128]{2,1,0:T(8,128)S(1)}, u32[]{:S(2)}, u32[]{:S(2)}) collective-permute-start(f32[38,8,128]{2,1,0:T(8,128)S(1)} %get-tuple-element.51), channel_id=1, source_target_pairs={{0,16},{16,32},{32,48},{48,64},{64,80},{80,96},{96,112},{112,0},{1... | collective-permute-start | bytes 466952 | tf_op jit(solution)/shard_map/ppermute | solution.py:638
  10.2 2.7 %collective-permute-start.10 = (f32[16,16,128]{2,1,0:T(8,128)S(1)}, f32[16,16,128]{2,1,0:T(8,128)S(1)}, u32[]{:S(2)}, u32[]{:S(2)}) collective-permute-start(f32[16,16,128]{2,1,0:T(8,128)S(1)} %get-tuple-element.70), channel_id=1, source_target_pairs={{0,1},{1,0},{2,3},{3,2},{4,5},{5,4},{6,7},{7,6},{8,9},{9,8},{10,11... | collective-permute-start | bytes 393224 | tf_op jit(solution)/shard_map/ppermute | solution.py:638
  13.0 0.5 shard_map.41
  13.5 1.4 %collective-permute-done.2.from_right = f32[38,8,128]{2,1,0:T(8,128)S(1)} collective-permute-done((f32[38,8,128]{2,1,0:T(8,128)S(1)}, f32[38,8,128]{2,1,0:T(8,128)S(1)}, u32[]{:S(2)}, u32[]{:S(2)}) %collective-permute-start.2) | collective-permute-done | bytes 155680 | tf_op jit(solution)/shard_map/ppermute | solution.py:638
  14.9 0.3 shard_map.42
  15.2 1.3 %collective-permute-start.3 = (f32[3,40,128]{2,1,0:T(8,128)S(1)}, f32[3,40,128]{2,1,0:T(8,128)S(1)}, u32[]{:S(2)}, u32[]{:S(2)}) collective-permute-start(f32[3,40,128]{2,1,0:T(8,128)S(1)} %get-tuple-element.62), channel_id=1, source_target_pairs={{0,2},{2,4},{4,6},{6,8},{8,10},{10,12},{12,14},{14,0},{1,3},{3,5},... | collective-permute-start | bytes 184328 | tf_op jit(solution)/shard_map/ppermute | solution.py:638
  16.5 3.6 %collective-permute-start.4 = (f32[3,40,128]{2,1,0:T(8,128)S(1)}, f32[3,40,128]{2,1,0:T(8,128)S(1)}, u32[]{:S(2)}, u32[]{:S(2)}) collective-permute-start(f32[3,40,128]{2,1,0:T(8,128)S(1)} %get-tuple-element.63), channel_id=1, source_target_pairs={{0,14},{2,0},{4,2},{6,4},{8,6},{10,8},{12,10},{14,12},{1,15},{3,1}... | collective-permute-start | bytes 184328 | tf_op jit(solution)/shard_map/ppermute | solution.py:638
  20.1 0.2 shard_map.40
  20.3 0.2 shard_map.45
  20.6 3.6 %collective-permute-start.12 = (f32[7,16,128]{2,1,0:T(8,128)S(1)}, f32[7,16,128]{2,1,0:T(8,128)S(1)}, u32[]{:S(2)}, u32[]{:S(2)}) collective-permute-start(f32[7,16,128]{2,1,0:T(8,128)S(1)} %get-tuple-element.74), channel_id=1, source_target_pairs={{0,14},{2,0},{4,2},{6,4},{8,6},{10,8},{12,10},{14,12},{1,15},{3,1}... | collective-permute-start | bytes 172040 | tf_op jit(solution)/shard_map/ppermute | solution.py:638
  24.2 1.4 %shard_map.43 = (f32[6,40,128]{2,1,0:T(8,128)S(1)}, f32[6,40,128]{2,1,0:T(8,128)S(1)}, f32[6,40,128]{2,1,0:T(8,128)S(1)}, f32[38,40,128]{2,1,0:T(8,128)S(1)}, f3...) custom-call(f32[32,32,128]{2,1,0:T(8,128)S(1)} %copy-done.2, f32[38,40,128]{2,1,0:T(8,128)S(1)} %get-tuple-element.53.gm, ...), custom_call_target="tpu_custom_call" | custom-call | bytes 7000000 | tf_op jit(solution)/shard_map/pallas_call | solution.py:37
  25.6 2.5 %collective-permute-start.5 = (f32[8,16,128]{2,1,0:T(8,128)S(1)}, f32[8,16,128]{2,1,0:T(8,128)S(1)}, u32[]{:S(2)}, u32[]{:S(2)}) collective-permute-start(f32[8,16,128]{2,1,0:T(8,128)S(1)} %get-tuple-element.64), channel_id=1, source_target_pairs={{0,1},{1,0},{2,3},{3,2},{4,5},{5,4},{6,7},{7,6},{8,9},{9,8},{10,11... | collective-permute-start | bytes 196616 | tf_op jit(solution)/shard_map/ppermute | solution.py:638
  28.2 1.2 %collective-permute-start.14 = (f32[46,16,128]{2,1,0:T(8,128)S(1)}, f32[46,16,128]{2,1,0:T(8,128)S(1)}, u32[]{:S(2)}, u32[]{:S(2)}) collective-permute-start(f32[46,16,128]{2,1,0:T(8,128)S(1)} %pad_maximum_fusion.own), channel_id=1, source_target_pairs={{0,112},{16,0},{32,16},{48,32},{64,48},{80,64},{96,80},{112,96},{1... | collective-permute-start | bytes 1130504 | tf_op jit(solution)/shard_map/ppermute | solution.py:638
  29.3 0.6 collective-permute-start.13
  29.9 0.4 collective-permute-done.5
  30.5 3.6 %collective-permute-start.7 = (f32[4,16,128]{2,1,0:T(8,128)S(1)}, f32[4,16,128]{2,1,0:T(8,128)S(1)}, u32[]{:S(2)}, u32[]{:S(2)}) collective-permute-start(f32[4,16,128]{2,1,0:T(8,128)S(1)} %get-tuple-element.67), channel_id=1, source_target_pairs={{0,14},{2,0},{4,2},{6,4},{8,6},{10,8},{12,10},{14,12},{1,15},{3,1}... | collective-permute-start | bytes 98312 | tf_op jit(solution)/shard_map/ppermute | solution.py:638
  34.1 1.3 %collective-permute-done.6 = f32[4,16,128]{2,1,0:T(8,128)S(1)} collective-permute-done((f32[4,16,128]{2,1,0:T(8,128)S(1)}, f32[4,16,128]{2,1,0:T(8,128)S(1)}, u32[]{:S(2)}, u32[]{:S(2)}) %collective-permute-start.6) | collective-permute-done | bytes 32800 | tf_op jit(solution)/shard_map/ppermute | solution.py:638
  35.4 3.2 %collective-permute-start.9 = (f32[24,16,128]{2,1,0:T(8,128)S(1)}, f32[24,16,128]{2,1,0:T(8,128)S(1)}, u32[]{:S(2)}, u32[]{:S(2)}) collective-permute-start(f32[24,16,128]{2,1,0:T(8,128)S(1)} %constant_dynamic-update-slice_fusion.own), channel_id=1, source_target_pairs={{0,112},{16,0},{32,16},{48,32},{64,48},{80,64},{96,80},{112,96},{1... | collective-permute-start | bytes 589832 | tf_op jit(solution)/shard_map/ppermute | solution.py:638
  38.6 0.6 collective-permute-start.8
  39.2 1.3 %shard_map.46 = (f32[32,40,128]{2,1,0:T(8,128)S(1)}, f32[32,40,128]{2,1,0:T(8,128)S(1)}, f32[32,40,128]{2,1,0:T(8,128)S(1)}, f32[16,24,128]{2,1,0:T(8,128)S(1)},...) custom-call(f32[46,16,128]{2,1,0:T(8,128)S(1)} %pad_maximum_fusion.own, ...), custom_call_target="tpu_custom_call" | custom-call | bytes 7000000 | tf_op jit(solution)/shard_map/pallas_call | solution.py:37
  40.5 2.0 %collective-permute-done.9.xr = f32[24,16,128]{2,1,0:T(8,128)S(1)} collective-permute-done((f32[24,16,128]{2,1,0:T(8,128)S(1)}, f32[24,16,128]{2,1,0:T(8,128)S(1)}, u32[]{:S(2)}, u32[]{:S(2)}) %collective-permute-start.9) | collective-permute-done | bytes 196640 | tf_op jit(solution)/shard_map/ppermute | solution.py:638
  42.5 2.1 %shard_map.47 = (f32[34,40,128]{2,1,0:T(8,128)S(1)}, f32[34,40,128]{2,1,0:T(8,128)S(1)}, f32[16,24,128]{2,1,0:T(8,128)S(1)}, f32[16,24,128]{2,1,0:T(8,128)S(1)}, f32[192,4,128]{2,1,0:T(4,128)S(1)}) custom-call(f32[24,16,128]{2,1,0:T(8,128)S(1)} %constant_dynamic-update-slice_fusion.own, f32[24,16,128]{2,1,0:T(8,128)S(1)} %collective-permute-done.8.xl, ...), custom_call_target="tpu_custom_call" | custom-call | bytes 10500000 | tf_op jit(solution)/shard_map/pallas_call | solution.py:37
  44.7 19.7 %all_to_all.5.gathered = f32[192,4,128]{2,1,0:T(4,128)S(1)} all-to-all(f32[192,4,128]{2,1,0:T(4,128)S(1)} %get-tuple-element.83), channel_id=1, replica_groups=mesh['gx'=8,'gy'=8,'gz'=2] {'gx','gy'}, dimensions={0} | all-to-all | bytes 786432 | tf_op jit(solution)/shard_map/all_to_all | solution.py:695
  64.4 1.9 %shard_map.48.u3 = f32[8,32,128]{2,1,0:T(8,128)S(1)} custom-call(f32[192,4,128]{2,1,0:T(4,128)S(1)} %all_to_all.5.gathered), custom_call_target="tpu_custom_call" | custom-call | bytes 7000000 | tf_op jit(solution)/shard_map/pallas_call | solution.py:37
  66.3 0.5 shard_map.49.u2
  66.8 1.0 %shard_map.50.u1 = f32[34,40,128]{2,1,0:T(8,128)S(1)} custom-call(f32[16,24,128]{2,1,0:T(8,128)S(1)} %shard_map.49.u2, f32[34,40,128]{2,1,0:T(8,128)S(1)} %get-tuple-element.86.g1, f32[32,40,128]{2,1,0:T(8,128)S(1)} %get-tuple-element.77.c1, f32[32,40,128]{2,1,0:T(8,128)S(1)} %get-tuple-element.76.s1, f32[34,40,128]{2,1,0:T(8,128)S(1)} %get-tuple-element.87.q1), custom_call_target="tpu_custom_call" | custom-call | bytes 5250000 | tf_op jit(solution)/shard_map/pallas_call | solution.py:37
  67.8 2.4 %shard_map.51 = f32[32,32,128]{2,1,0:T(8,128)} custom-call(f32[34,40,128]{2,1,0:T(8,128)S(1)} %shard_map.50.u1, f32[38,40,128]{2,1,0:T(8,128)S(1)} %get-tuple-element.53.gm, f32[38,40,128]{2,1,0:T(8,128)S(1)} %get-tuple-element.54.cm, f32[38,40,128]{2,1,0:T(8,128)S(1)} %get-tuple-element.55.sm, f32[38,40,128]{2,1,0:T(8,128)S(1)} %get-tuple-element.88.q, ...), custom_call_target="tpu_custom_call" | custom-call | bytes 8750000 | tf_op jit(solution)/shard_map/pallas_call | solution.py:37
  (29 shorter events, 0.5 us)
Async XLA Ops:
  0.0 4.6 %copy-start = (f32[32,32,128]{2,1,0:T(8,128)S(1)}, f32[32,32,128]{2,1,0:T(8,128)}, u32[]{:S(2)}) copy-start(f32[32,32,128]{2,1,0:T(8,128)} %s.7) | copy-start | bytes 1572868
  1.0 6.2 %collective-permute-start = (f32[7,32,128]{2,1,0:T(8,128)S(1)}, f32[7,32,128]{2,1,0:T(8,128)S(1)}, u32[]{:S(2)}, u32[]{:S(2)}) collective-permute-start(f32[7,32,128]{2,1,0:T(8,128)S(1)} %shard_map.38), channel_id=1, source_target_pairs={{0,1},{1,0},{2,3},{3,2},{4,5},{5,4},{6,7},{7,6},{8,9},{9,8},{10,11... | collective-permute-start | bytes 344072 | tf_op jit(solution)/shard_map/ppermute | solution.py:638
  4.6 1.0 %copy-start.1 = (f32[32,32,128]{2,1,0:T(8,128)S(1)}, f32[32,32,128]{2,1,0:T(8,128)}, u32[]{:S(2)}) copy-start(f32[32,32,128]{2,1,0:T(8,128)} %f.3) | copy-start | bytes 1572868
  5.7 1.0 %copy-start.3 = (f32[32,32,128]{2,1,0:T(8,128)S(1)}, f32[32,32,128]{2,1,0:T(8,128)}, u32[]{:S(2)}) copy-start(f32[32,32,128]{2,1,0:T(8,128)} %k.1) | copy-start | bytes 1572868
  7.3 6.2 %collective-permute-start.1 = (f32[38,8,128]{2,1,0:T(8,128)S(1)}, f32[38,8,128]{2,1,0:T(8,128)S(1)}, u32[]{:S(2)}, u32[]{:S(2)}) collective-permute-start(f32[38,8,128]{2,1,0:T(8,128)S(1)} %get-tuple-element.51), channel_id=1, source_target_pairs={{0,16},{16,32},{32,48},{48,64},{64,80},{80,96},{96,112},{112,0},{1... | collective-permute-start | bytes 466952 | tf_op jit(solution)/shard_map/ppermute | solution.py:638
  10.2 4.7 %collective-permute-start.2 = (f32[38,8,128]{2,1,0:T(8,128)S(1)}, f32[38,8,128]{2,1,0:T(8,128)S(1)}, u32[]{:S(2)}, u32[]{:S(2)}) collective-permute-start(f32[38,8,128]{2,1,0:T(8,128)S(1)} %get-tuple-element.52), channel_id=1, source_target_pairs={{0,112},{16,0},{32,16},{48,32},{64,48},{80,64},{96,80},{112,96},{1... | collective-permute-start | bytes 466952 | tf_op jit(solution)/shard_map/ppermute | solution.py:638
  10.2 10.0 %collective-permute-start.10 = (f32[16,16,128]{2,1,0:T(8,128)S(1)}, f32[16,16,128]{2,1,0:T(8,128)S(1)}, u32[]{:S(2)}, u32[]{:S(2)}) collective-permute-start(f32[16,16,128]{2,1,0:T(8,128)S(1)} %get-tuple-element.70), channel_id=1, source_target_pairs={{0,1},{1,0},{2,3},{3,2},{4,5},{5,4},{6,7},{7,6},{8,9},{9,8},{10,11... | collective-permute-start | bytes 393224 | tf_op jit(solution)/shard_map/ppermute | solution.py:638
  15.2 8.9 %collective-permute-start.3 = (f32[3,40,128]{2,1,0:T(8,128)S(1)}, f32[3,40,128]{2,1,0:T(8,128)S(1)}, u32[]{:S(2)}, u32[]{:S(2)}) collective-permute-start(f32[3,40,128]{2,1,0:T(8,128)S(1)} %get-tuple-element.62), channel_id=1, source_target_pairs={{0,2},{2,4},{4,6},{6,8},{8,10},{10,12},{12,14},{14,0},{1,3},{3,5},... | collective-permute-start | bytes 184328 | tf_op jit(solution)/shard_map/ppermute | solution.py:638
  16.5 7.6 %collective-permute-start.4 = (f32[3,40,128]{2,1,0:T(8,128)S(1)}, f32[3,40,128]{2,1,0:T(8,128)S(1)}, u32[]{:S(2)}, u32[]{:S(2)}) collective-permute-start(f32[3,40,128]{2,1,0:T(8,128)S(1)} %get-tuple-element.63), channel_id=1, source_target_pairs={{0,14},{2,0},{4,2},{6,4},{8,6},{10,8},{12,10},{14,12},{1,15},{3,1}... | collective-permute-start | bytes 184328 | tf_op jit(solution)/shard_map/ppermute | solution.py:638
  20.2 3.9 %copy-start.2 = (f32[32,32,128]{2,1,0:T(8,128)S(1)}, f32[32,32,128]{2,1,0:T(8,128)}, u32[]{:S(2)}) copy-start(f32[32,32,128]{2,1,0:T(8,128)} %f.3) | copy-start | bytes 1572868
  20.5 7.6 %collective-permute-start.11 = (f32[7,16,128]{2,1,0:T(8,128)S(1)}, f32[7,16,128]{2,1,0:T(8,128)S(1)}, u32[]{:S(2)}, u32[]{:S(2)}) collective-permute-start(f32[7,16,128]{2,1,0:T(8,128)S(1)} %get-tuple-element.73), channel_id=1, source_target_pairs={{0,2},{2,4},{4,6},{6,8},{8,10},{10,12},{12,14},{14,0},{1,3},{3,5},... | collective-permute-start | bytes 172040 | tf_op jit(solution)/shard_map/ppermute | solution.py:638
  20.6 7.6 %collective-permute-start.12 = (f32[7,16,128]{2,1,0:T(8,128)S(1)}, f32[7,16,128]{2,1,0:T(8,128)S(1)}, u32[]{:S(2)}, u32[]{:S(2)}) collective-permute-start(f32[7,16,128]{2,1,0:T(8,128)S(1)} %get-tuple-element.74), channel_id=1, source_target_pairs={{0,14},{2,0},{4,2},{6,4},{8,6},{10,8},{12,10},{14,12},{1,15},{3,1}... | collective-permute-start | bytes 172040 | tf_op jit(solution)/shard_map/ppermute | solution.py:638
  25.6 4.7 %collective-permute-start.5 = (f32[8,16,128]{2,1,0:T(8,128)S(1)}, f32[8,16,128]{2,1,0:T(8,128)S(1)}, u32[]{:S(2)}, u32[]{:S(2)}) collective-permute-start(f32[8,16,128]{2,1,0:T(8,128)S(1)} %get-tuple-element.64), channel_id=1, source_target_pairs={{0,1},{1,0},{2,3},{3,2},{4,5},{5,4},{6,7},{7,6},{8,9},{9,8},{10,11... | collective-permute-start | bytes 196616 | tf_op jit(solution)/shard_map/ppermute | solution.py:638
  28.2 11.0 %collective-permute-start.14 = (f32[46,16,128]{2,1,0:T(8,128)S(1)}, f32[46,16,128]{2,1,0:T(8,128)S(1)}, u32[]{:S(2)}, u32[]{:S(2)}) collective-permute-start(f32[46,16,128]{2,1,0:T(8,128)S(1)} %pad_maximum_fusion.own), channel_id=1, source_target_pairs={{0,112},{16,0},{32,16},{48,32},{64,48},{80,64},{96,80},{112,96},{1... | collective-permute-start | bytes 1130504 | tf_op jit(solution)/shard_map/ppermute | solution.py:638
  29.3 9.8 %collective-permute-start.13 = (f32[46,16,128]{2,1,0:T(8,128)S(1)}, f32[46,16,128]{2,1,0:T(8,128)S(1)}, u32[]{:S(2)}, u32[]{:S(2)}) collective-permute-start(f32[46,16,128]{2,1,0:T(8,128)S(1)} %pad_maximum_fusion.own), channel_id=1, source_target_pairs={{0,16},{16,32},{32,48},{48,64},{64,80},{80,96},{96,112},{112,0},{1... | collective-permute-start | bytes 1130504 | tf_op jit(solution)/shard_map/ppermute | solution.py:638
  30.5 4.9 %collective-permute-start.6 = (f32[4,16,128]{2,1,0:T(8,128)S(1)}, f32[4,16,128]{2,1,0:T(8,128)S(1)}, u32[]{:S(2)}, u32[]{:S(2)}) collective-permute-start(f32[4,16,128]{2,1,0:T(8,128)S(1)} %get-tuple-element.66), channel_id=1, source_target_pairs={{0,2},{2,4},{4,6},{6,8},{8,10},{10,12},{12,14},{14,0},{1,3},{3,5},... | collective-permute-start | bytes 98312 | tf_op jit(solution)/shard_map/ppermute | solution.py:638
  30.5 4.9 %collective-permute-start.7 = (f32[4,16,128]{2,1,0:T(8,128)S(1)}, f32[4,16,128]{2,1,0:T(8,128)S(1)}, u32[]{:S(2)}, u32[]{:S(2)}) collective-permute-start(f32[4,16,128]{2,1,0:T(8,128)S(1)} %get-tuple-element.67), channel_id=1, source_target_pairs={{0,14},{2,0},{4,2},{6,4},{8,6},{10,8},{12,10},{14,12},{1,15},{3,1}... | collective-permute-start | bytes 98312 | tf_op jit(solution)/shard_map/ppermute | solution.py:638
  35.4 7.1 %collective-permute-start.9 = (f32[24,16,128]{2,1,0:T(8,128)S(1)}, f32[24,16,128]{2,1,0:T(8,128)S(1)}, u32[]{:S(2)}, u32[]{:S(2)}) collective-permute-start(f32[24,16,128]{2,1,0:T(8,128)S(1)} %constant_dynamic-update-slice_fusion.own), channel_id=1, source_target_pairs={{0,112},{16,0},{32,16},{48,32},{64,48},{80,64},{96,80},{112,96},{1... | collective-permute-start | bytes 589832 | tf_op jit(solution)/shard_map/ppermute | solution.py:638
  38.6 3.9 %collective-permute-start.8 = (f32[24,16,128]{2,1,0:T(8,128)S(1)}, f32[24,16,128]{2,1,0:T(8,128)S(1)}, u32[]{:S(2)}, u32[]{:S(2)}) collective-permute-start(f32[24,16,128]{2,1,0:T(8,128)S(1)} %constant_dynamic-update-slice_fusion.own), channel_id=1, source_target_pairs={{0,16},{16,32},{32,48},{48,64},{64,80},{80,96},{96,112},{112,0},{1... | collective-permute-start | bytes 589832 | tf_op jit(solution)/shard_map/ppermute | solution.py:638

commit v2 on v1

--- a/solution.py
+++ b/solution.py
@@ -447,12 +447,14 @@
     parts = [level3_rows(ev, e2, r2), sk3[:4], sk3[4:]]
     parts = [pltpu.roll(part, 16 * iy, 1) for part in parts]
 
+    tiles = [jnp.concatenate([parts[i], parts[(i + 1) % 3]], axis=0) for i in (0, 2, 1)]
+
     def copy(n, _):
         for i in range(3):
-            chunk[3 * n + i] = parts[i]
+            chunk[3 * n + i] = tiles[i]
         return 0
 
-    lax.fori_loop(0, 64, copy, 0, unroll=8)
+    lax.fori_loop(0, 32, copy, 0, unroll=8)
 
 
 def spread_in(shape, last):
@@ -689,10 +691,11 @@
     g1, q1, g2, q2, chunk = run(
         k_down12,
         (f1, *pair(f1, f1, "gx"), s1, c1, w1, s2, c2, w2, sk3),
-        [(34, 40, 128)] * 2 + [(16, 24, 128)] * 2 + [(192, 4, 128)],
+        [(34, 40, 128)] * 2 + [(16, 24, 128)] * 2 + [(96, 8, 128)],
         [(32, 40, 128), (16, 40, 128), (16, 24, 128), (8, 8, 128), (32, 128)],
     )
-    gathered = lax.all_to_all(chunk, ("gx", "gy"), 0, 0, tiled=True)
+    gathered = lax.all_to_all(chunk.reshape(64, 1, 1536), ("gx", "gy"), 0, 0, tiled=True)
+    gathered = gathered.reshape(192, 4, 128)
     (u3,) = run(
         k_whole, (gathered,), [(8, 32, 128)], [(3, 8, 32, 128), (4, 32, 128), (4, 32, 128)]
     )

time: 70.6 us -> 70.6 us (level)
  no operation moved by 1% of the time
where the time goes in v2:
time: 70.6 us; the launch traced here: 70.3 us
  starting transfers between devices  29.5 us (42%)
  blocking collectives  19.7 us (28%)
  Pallas kernels  12.7 us (18%)
  waiting for transfers between devices  5.02 us (7%)
  local copies, waits for them, and re-layouts  2.11 us (3%)
  other arithmetic  0.98 us (1%)
    ppermute x15, starting transfers between devices, ring(): return lax.ppermute(v, axis, [(i, (i + step) % n) for i in range(n)])  29.5 us
    all_to_all x1, blocking collectives, shards(): lax.all_to_all(chunk.reshape(64, 1, 1536), ('gx', 'gy'), 0, 0, tiled=True)  19.7 us
    pallas_call x15, Pallas kernels, run(): pl.pallas_call(body, out_shape=[jax.ShapeDtypeStruct(o, F32) for o in out...  12.7 us
    ppermute x15, waiting for transfers between devices, ring(): return lax.ppermute(v, axis, [(i, (i + step) % n) for i in range(n)])  5.02 us
    unnamed x10, local copies, waits for them, and re-layouts  2.11 us
  transfers between devices with their start and end apart: 15, of which 4 were waited for; matrix products, arithmetic and copies ran while one was open for 0% of the time, Pallas kernels for 7%

profile of v2, /device:TPU:1, one launch (start us, length us, event | category | flops | bytes accessed | tf_op | source)
XLA Modules:
  0.0 70.3 jit_solution(4035830572694879060)
XLA Ops:
  0.0 0.9 %compare_select_fusion.1 = (f32[3,32,128]{2,1,0:T(8,128)S(1)}, f32[3,32,128]{2,1,0:T(8,128)S(1)}, f32[3,32,128]{2,1,0:T(8,128)S(1)}) fusion(f32[32,32,128]{2,1,0:T(8,128)} %k.1, s32[]{:T(128)S(6)} %select_n.14, f32[32,32,128]{2,1,0:T(8,128)} %s.7, f32[32,32,128]{2,1,0:T(8,128)} %f.3), kind=kLoop, calls=%fused_computation.7 | loop fusion | flops 135168 | bytes 294916 | tf_op jit(solution)/shard_map/jit(_where)/select_n | solution.py:661
  1.0 3.7 %collective-permute-start = (f32[7,32,128]{2,1,0:T(8,128)S(1)}, f32[7,32,128]{2,1,0:T(8,128)S(1)}, u32[]{:S(2)}, u32[]{:S(2)}) collective-permute-start(f32[7,32,128]{2,1,0:T(8,128)S(1)} %shard_map.38), channel_id=1, source_target_pairs={{0,1},{1,0},{2,3},{3,2},{4,5},{5,4},{6,7},{7,6},{8,9},{9,8},{10,11... | collective-permute-start | bytes 344072 | tf_op jit(solution)/shard_map/ppermute | solution.py:640
  4.6 1.0 %copy-done.1 = f32[32,32,128]{2,1,0:T(8,128)S(1)} copy-done((f32[32,32,128]{2,1,0:T(8,128)S(1)}, f32[32,32,128]{2,1,0:T(8,128)}, u32[]{:S(2)}) %copy-start.1) | copy-done | bytes 524312
  5.7 1.0 %copy-done.3 = f32[32,32,128]{2,1,0:T(8,128)S(1)} copy-done((f32[32,32,128]{2,1,0:T(8,128)S(1)}, f32[32,32,128]{2,1,0:T(8,128)}, u32[]{:S(2)}) %copy-start.3) | copy-done | bytes 524312
  6.7 0.5 shard_map.37
  7.3 2.9 %collective-permute-start.1 = (f32[38,8,128]{2,1,0:T(8,128)S(1)}, f32[38,8,128]{2,1,0:T(8,128)S(1)}, u32[]{:S(2)}, u32[]{:S(2)}) collective-permute-start(f32[38,8,128]{2,1,0:T(8,128)S(1)} %get-tuple-element.51), channel_id=1, source_target_pairs={{0,16},{16,32},{32,48},{48,64},{64,80},{80,96},{96,112},{112,0},{1... | collective-permute-start | bytes 466952 | tf_op jit(solution)/shard_map/ppermute | solution.py:640
  10.2 2.7 %collective-permute-start.10 = (f32[16,16,128]{2,1,0:T(8,128)S(1)}, f32[16,16,128]{2,1,0:T(8,128)S(1)}, u32[]{:S(2)}, u32[]{:S(2)}) collective-permute-start(f32[16,16,128]{2,1,0:T(8,128)S(1)} %get-tuple-element.70), channel_id=1, source_target_pairs={{0,1},{1,0},{2,3},{3,2},{4,5},{5,4},{6,7},{7,6},{8,9},{9,8},{10,11... | collective-permute-start | bytes 393224 | tf_op jit(solution)/shard_map/ppermute | solution.py:640
  13.0 0.5 shard_map.41
  13.5 1.4 %collective-permute-done.2.from_right = f32[38,8,128]{2,1,0:T(8,128)S(1)} collective-permute-done((f32[38,8,128]{2,1,0:T(8,128)S(1)}, f32[38,8,128]{2,1,0:T(8,128)S(1)}, u32[]{:S(2)}, u32[]{:S(2)}) %collective-permute-start.2) | collective-permute-done | bytes 155680 | tf_op jit(solution)/shard_map/ppermute | solution.py:640
  14.9 0.3 shard_map.42
  15.2 1.3 %collective-permute-start.3 = (f32[3,40,128]{2,1,0:T(8,128)S(1)}, f32[3,40,128]{2,1,0:T(8,128)S(1)}, u32[]{:S(2)}, u32[]{:S(2)}) collective-permute-start(f32[3,40,128]{2,1,0:T(8,128)S(1)} %get-tuple-element.62), channel_id=1, source_target_pairs={{0,2},{2,4},{4,6},{6,8},{8,10},{10,12},{12,14},{14,0},{1,3},{3,5},... | collective-permute-start | bytes 184328 | tf_op jit(solution)/shard_map/ppermute | solution.py:640
  16.5 3.6 %collective-permute-start.4 = (f32[3,40,128]{2,1,0:T(8,128)S(1)}, f32[3,40,128]{2,1,0:T(8,128)S(1)}, u32[]{:S(2)}, u32[]{:S(2)}) collective-permute-start(f32[3,40,128]{2,1,0:T(8,128)S(1)} %get-tuple-element.63), channel_id=1, source_target_pairs={{0,14},{2,0},{4,2},{6,4},{8,6},{10,8},{12,10},{14,12},{1,15},{3,1}... | collective-permute-start | bytes 184328 | tf_op jit(solution)/shard_map/ppermute | solution.py:640
  20.1 0.2 shard_map.40
  20.3 0.2 shard_map.45
  20.6 3.6 %collective-permute-start.12 = (f32[7,16,128]{2,1,0:T(8,128)S(1)}, f32[7,16,128]{2,1,0:T(8,128)S(1)}, u32[]{:S(2)}, u32[]{:S(2)}) collective-permute-start(f32[7,16,128]{2,1,0:T(8,128)S(1)} %get-tuple-element.74), channel_id=1, source_target_pairs={{0,14},{2,0},{4,2},{6,4},{8,6},{10,8},{12,10},{14,12},{1,15},{3,1}... | collective-permute-start | bytes 172040 | tf_op jit(solution)/shard_map/ppermute | solution.py:640
  24.2 1.4 %shard_map.43 = (f32[6,40,128]{2,1,0:T(8,128)S(1)}, f32[6,40,128]{2,1,0:T(8,128)S(1)}, f32[6,40,128]{2,1,0:T(8,128)S(1)}, f32[38,40,128]{2,1,0:T(8,128)S(1)}, f3...) custom-call(f32[32,32,128]{2,1,0:T(8,128)S(1)} %copy-done.2, f32[38,40,128]{2,1,0:T(8,128)S(1)} %get-tuple-element.53.gm, ...), custom_call_target="tpu_custom_call" | custom-call | bytes 7000000 | tf_op jit(solution)/shard_map/pallas_call | solution.py:37
  25.6 2.5 %collective-permute-start.5 = (f32[8,16,128]{2,1,0:T(8,128)S(1)}, f32[8,16,128]{2,1,0:T(8,128)S(1)}, u32[]{:S(2)}, u32[]{:S(2)}) collective-permute-start(f32[8,16,128]{2,1,0:T(8,128)S(1)} %get-tuple-element.64), channel_id=1, source_target_pairs={{0,1},{1,0},{2,3},{3,2},{4,5},{5,4},{6,7},{7,6},{8,9},{9,8},{10,11... | collective-permute-start | bytes 196616 | tf_op jit(solution)/shard_map/ppermute | solution.py:640
  28.2 1.2 %collective-permute-start.14 = (f32[46,16,128]{2,1,0:T(8,128)S(1)}, f32[46,16,128]{2,1,0:T(8,128)S(1)}, u32[]{:S(2)}, u32[]{:S(2)}) collective-permute-start(f32[46,16,128]{2,1,0:T(8,128)S(1)} %pad_maximum_fusion.own), channel_id=1, source_target_pairs={{0,112},{16,0},{32,16},{48,32},{64,48},{80,64},{96,80},{112,96},{1... | collective-permute-start | bytes 1130504 | tf_op jit(solution)/shard_map/ppermute | solution.py:640
  29.3 0.6 collective-permute-start.13
  29.9 0.4 collective-permute-done.5
  30.5 3.6 %collective-permute-start.7 = (f32[4,16,128]{2,1,0:T(8,128)S(1)}, f32[4,16,128]{2,1,0:T(8,128)S(1)}, u32[]{:S(2)}, u32[]{:S(2)}) collective-permute-start(f32[4,16,128]{2,1,0:T(8,128)S(1)} %get-tuple-element.67), channel_id=1, source_target_pairs={{0,14},{2,0},{4,2},{6,4},{8,6},{10,8},{12,10},{14,12},{1,15},{3,1}... | collective-permute-start | bytes 98312 | tf_op jit(solution)/shard_map/ppermute | solution.py:640
  34.1 1.3 %collective-permute-done.6 = f32[4,16,128]{2,1,0:T(8,128)S(1)} collective-permute-done((f32[4,16,128]{2,1,0:T(8,128)S(1)}, f32[4,16,128]{2,1,0:T(8,128)S(1)}, u32[]{:S(2)}, u32[]{:S(2)}) %collective-permute-start.6) | collective-permute-done | bytes 32800 | tf_op jit(solution)/shard_map/ppermute | solution.py:640
  35.4 3.2 %collective-permute-start.9 = (f32[24,16,128]{2,1,0:T(8,128)S(1)}, f32[24,16,128]{2,1,0:T(8,128)S(1)}, u32[]{:S(2)}, u32[]{:S(2)}) collective-permute-start(f32[24,16,128]{2,1,0:T(8,128)S(1)} %constant_dynamic-update-slice_fusion.own), channel_id=1, source_target_pairs={{0,112},{16,0},{32,16},{48,32},{64,48},{80,64},{96,80},{112,96},{1... | collective-permute-start | bytes 589832 | tf_op jit(solution)/shard_map/ppermute | solution.py:640
  38.6 0.6 collective-permute-start.8
  39.2 1.3 %shard_map.46 = (f32[32,40,128]{2,1,0:T(8,128)S(1)}, f32[32,40,128]{2,1,0:T(8,128)S(1)}, f32[32,40,128]{2,1,0:T(8,128)S(1)}, f32[16,24,128]{2,1,0:T(8,128)S(1)},...) custom-call(f32[46,16,128]{2,1,0:T(8,128)S(1)} %pad_maximum_fusion.own, ...), custom_call_target="tpu_custom_call" | custom-call | bytes 7000000 | tf_op jit(solution)/shard_map/pallas_call | solution.py:37
  40.5 2.0 %collective-permute-done.9.xr = f32[24,16,128]{2,1,0:T(8,128)S(1)} collective-permute-done((f32[24,16,128]{2,1,0:T(8,128)S(1)}, f32[24,16,128]{2,1,0:T(8,128)S(1)}, u32[]{:S(2)}, u32[]{:S(2)}) %collective-permute-start.9) | collective-permute-done | bytes 196640 | tf_op jit(solution)/shard_map/ppermute | solution.py:640
  42.5 2.1 %shard_map.47 = (f32[34,40,128]{2,1,0:T(8,128)S(1)}, f32[34,40,128]{2,1,0:T(8,128)S(1)}, f32[16,24,128]{2,1,0:T(8,128)S(1)}, f32[16,24,128]{2,1,0:T(8,128)S(1)}, f32[96,8,128]{2,1,0:T(8,128)S(1)}) custom-call(f32[24,16,128]{2,1,0:T(8,128)S(1)} %constant_dynamic-update-slice_fusion.own, f32[24,16,128]{2,1,0:T(8,128)S(1)} %collective-permute-done.8.xl, ...), custom_call_target="tpu_custom_call" | custom-call | bytes 10500000 | tf_op jit(solution)/shard_map/pallas_call | solution.py:37
  44.6 19.7 %all_to_all.5 = f32[64,1,1536]{2,1,0:T(1,128)S(1)} all-to-all(f32[64,1,1536]{2,1,0:T(1,128)S(1)} %bitcast.3), channel_id=1, replica_groups=mesh['gx'=8,'gy'=8,'gz'=2] {'gx','gy'}, dimensions={0} | all-to-all | bytes 786432 | tf_op jit(solution)/shard_map/all_to_all | solution.py:697
  64.4 1.9 %shard_map.48.u3 = f32[8,32,128]{2,1,0:T(8,128)S(1)} custom-call(f32[192,4,128]{2,1,0:T(4,128)S(1)} %bitcast.2), custom_call_target="tpu_custom_call" | custom-call | bytes 7000000 | tf_op jit(solution)/shard_map/pallas_call | solution.py:37
  66.2 0.5 shard_map.49.u2
  66.8 1.0 %shard_map.50.u1 = f32[34,40,128]{2,1,0:T(8,128)S(1)} custom-call(f32[16,24,128]{2,1,0:T(8,128)S(1)} %shard_map.49.u2, f32[34,40,128]{2,1,0:T(8,128)S(1)} %get-tuple-element.86.g1, f32[32,40,128]{2,1,0:T(8,128)S(1)} %get-tuple-element.77.c1, f32[32,40,128]{2,1,0:T(8,128)S(1)} %get-tuple-element.76.s1, f32[34,40,128]{2,1,0:T(8,128)S(1)} %get-tuple-element.87.q1), custom_call_target="tpu_custom_call" | custom-call | bytes 5250000 | tf_op jit(solution)/shard_map/pallas_call | solution.py:37
  67.8 2.4 %shard_map.51 = f32[32,32,128]{2,1,0:T(8,128)} custom-call(f32[34,40,128]{2,1,0:T(8,128)S(1)} %shard_map.50.u1, f32[38,40,128]{2,1,0:T(8,128)S(1)} %get-tuple-element.53.gm, f32[38,40,128]{2,1,0:T(8,128)S(1)} %get-tuple-element.54.cm, f32[38,40,128]{2,1,0:T(8,128)S(1)} %get-tuple-element.55.sm, f32[38,40,128]{2,1,0:T(8,128)S(1)} %get-tuple-element.88.q, ...), custom_call_target="tpu_custom_call" | custom-call | bytes 8750000 | tf_op jit(solution)/shard_map/pallas_call | solution.py:37
  (29 shorter events, 0.5 us)
Async XLA Ops:
  0.0 4.6 %copy-start = (f32[32,32,128]{2,1,0:T(8,128)S(1)}, f32[32,32,128]{2,1,0:T(8,128)}, u32[]{:S(2)}) copy-start(f32[32,32,128]{2,1,0:T(8,128)} %s.7) | copy-start | bytes 1572868
  1.0 6.2 %collective-permute-start = (f32[7,32,128]{2,1,0:T(8,128)S(1)}, f32[7,32,128]{2,1,0:T(8,128)S(1)}, u32[]{:S(2)}, u32[]{:S(2)}) collective-permute-start(f32[7,32,128]{2,1,0:T(8,128)S(1)} %shard_map.38), channel_id=1, source_target_pairs={{0,1},{1,0},{2,3},{3,2},{4,5},{5,4},{6,7},{7,6},{8,9},{9,8},{10,11... | collective-permute-start | bytes 344072 | tf_op jit(solution)/shard_map/ppermute | solution.py:640
  4.6 1.0 %copy-start.1 = (f32[32,32,128]{2,1,0:T(8,128)S(1)}, f32[32,32,128]{2,1,0:T(8,128)}, u32[]{:S(2)}) copy-start(f32[32,32,128]{2,1,0:T(8,128)} %f.3) | copy-start | bytes 1572868
  5.7 1.0 %copy-start.3 = (f32[32,32,128]{2,1,0:T(8,128)S(1)}, f32[32,32,128]{2,1,0:T(8,128)}, u32[]{:S(2)}) copy-start(f32[32,32,128]{2,1,0:T(8,128)} %k.1) | copy-start | bytes 1572868
  7.3 6.2 %collective-permute-start.1 = (f32[38,8,128]{2,1,0:T(8,128)S(1)}, f32[38,8,128]{2,1,0:T(8,128)S(1)}, u32[]{:S(2)}, u32[]{:S(2)}) collective-permute-start(f32[38,8,128]{2,1,0:T(8,128)S(1)} %get-tuple-element.51), channel_id=1, source_target_pairs={{0,16},{16,32},{32,48},{48,64},{64,80},{80,96},{96,112},{112,0},{1... | collective-permute-start | bytes 466952 | tf_op jit(solution)/shard_map/ppermute | solution.py:640
  10.2 4.7 %collective-permute-start.2 = (f32[38,8,128]{2,1,0:T(8,128)S(1)}, f32[38,8,128]{2,1,0:T(8,128)S(1)}, u32[]{:S(2)}, u32[]{:S(2)}) collective-permute-start(f32[38,8,128]{2,1,0:T(8,128)S(1)} %get-tuple-element.52), channel_id=1, source_target_pairs={{0,112},{16,0},{32,16},{48,32},{64,48},{80,64},{96,80},{112,96},{1... | collective-permute-start | bytes 466952 | tf_op jit(solution)/shard_map/ppermute | solution.py:640
  10.2 10.0 %collective-permute-start.10 = (f32[16,16,128]{2,1,0:T(8,128)S(1)}, f32[16,16,128]{2,1,0:T(8,128)S(1)}, u32[]{:S(2)}, u32[]{:S(2)}) collective-permute-start(f32[16,16,128]{2,1,0:T(8,128)S(1)} %get-tuple-element.70), channel_id=1, source_target_pairs={{0,1},{1,0},{2,3},{3,2},{4,5},{5,4},{6,7},{7,6},{8,9},{9,8},{10,11... | collective-permute-start | bytes 393224 | tf_op jit(solution)/shard_map/ppermute | solution.py:640
  15.2 8.9 %collective-permute-start.3 = (f32[3,40,128]{2,1,0:T(8,128)S(1)}, f32[3,40,128]{2,1,0:T(8,128)S(1)}, u32[]{:S(2)}, u32[]{:S(2)}) collective-permute-start(f32[3,40,128]{2,1,0:T(8,128)S(1)} %get-tuple-element.62), channel_id=1, source_target_pairs={{0,2},{2,4},{4,6},{6,8},{8,10},{10,12},{12,14},{14,0},{1,3},{3,5},... | collective-permute-start | bytes 184328 | tf_op jit(solution)/shard_map/ppermute | solution.py:640
  16.5 7.6 %collective-permute-start.4 = (f32[3,40,128]{2,1,0:T(8,128)S(1)}, f32[3,40,128]{2,1,0:T(8,128)S(1)}, u32[]{:S(2)}, u32[]{:S(2)}) collective-permute-start(f32[3,40,128]{2,1,0:T(8,128)S(1)} %get-tuple-element.63), channel_id=1, source_target_pairs={{0,14},{2,0},{4,2},{6,4},{8,6},{10,8},{12,10},{14,12},{1,15},{3,1}... | collective-permute-start | bytes 184328 | tf_op jit(solution)/shard_map/ppermute | solution.py:640
  20.2 3.9 %copy-start.2 = (f32[32,32,128]{2,1,0:T(8,128)S(1)}, f32[32,32,128]{2,1,0:T(8,128)}, u32[]{:S(2)}) copy-start(f32[32,32,128]{2,1,0:T(8,128)} %f.3) | copy-start | bytes 1572868
  20.5 7.6 %collective-permute-start.11 = (f32[7,16,128]{2,1,0:T(8,128)S(1)}, f32[7,16,128]{2,1,0:T(8,128)S(1)}, u32[]{:S(2)}, u32[]{:S(2)}) collective-permute-start(f32[7,16,128]{2,1,0:T(8,128)S(1)} %get-tuple-element.73), channel_id=1, source_target_pairs={{0,2},{2,4},{4,6},{6,8},{8,10},{10,12},{12,14},{14,0},{1,3},{3,5},... | collective-permute-start | bytes 172040 | tf_op jit(solution)/shard_map/ppermute | solution.py:640
  20.6 7.6 %collective-permute-start.12 = (f32[7,16,128]{2,1,0:T(8,128)S(1)}, f32[7,16,128]{2,1,0:T(8,128)S(1)}, u32[]{:S(2)}, u32[]{:S(2)}) collective-permute-start(f32[7,16,128]{2,1,0:T(8,128)S(1)} %get-tuple-element.74), channel_id=1, source_target_pairs={{0,14},{2,0},{4,2},{6,4},{8,6},{10,8},{12,10},{14,12},{1,15},{3,1}... | collective-permute-start | bytes 172040 | tf_op jit(solution)/shard_map/ppermute | solution.py:640
  25.6 4.7 %collective-permute-start.5 = (f32[8,16,128]{2,1,0:T(8,128)S(1)}, f32[8,16,128]{2,1,0:T(8,128)S(1)}, u32[]{:S(2)}, u32[]{:S(2)}) collective-permute-start(f32[8,16,128]{2,1,0:T(8,128)S(1)} %get-tuple-element.64), channel_id=1, source_target_pairs={{0,1},{1,0},{2,3},{3,2},{4,5},{5,4},{6,7},{7,6},{8,9},{9,8},{10,11... | collective-permute-start | bytes 196616 | tf_op jit(solution)/shard_map/ppermute | solution.py:640
  28.2 11.0 %collective-permute-start.14 = (f32[46,16,128]{2,1,0:T(8,128)S(1)}, f32[46,16,128]{2,1,0:T(8,128)S(1)}, u32[]{:S(2)}, u32[]{:S(2)}) collective-permute-start(f32[46,16,128]{2,1,0:T(8,128)S(1)} %pad_maximum_fusion.own), channel_id=1, source_target_pairs={{0,112},{16,0},{32,16},{48,32},{64,48},{80,64},{96,80},{112,96},{1... | collective-permute-start | bytes 1130504 | tf_op jit(solution)/shard_map/ppermute | solution.py:640
  29.3 9.8 %collective-permute-start.13 = (f32[46,16,128]{2,1,0:T(8,128)S(1)}, f32[46,16,128]{2,1,0:T(8,128)S(1)}, u32[]{:S(2)}, u32[]{:S(2)}) collective-permute-start(f32[46,16,128]{2,1,0:T(8,128)S(1)} %pad_maximum_fusion.own), channel_id=1, source_target_pairs={{0,16},{16,32},{32,48},{48,64},{64,80},{80,96},{96,112},{112,0},{1... | collective-permute-start | bytes 1130504 | tf_op jit(solution)/shard_map/ppermute | solution.py:640
  30.5 4.9 %collective-permute-start.6 = (f32[4,16,128]{2,1,0:T(8,128)S(1)}, f32[4,16,128]{2,1,0:T(8,128)S(1)}, u32[]{:S(2)}, u32[]{:S(2)}) collective-permute-start(f32[4,16,128]{2,1,0:T(8,128)S(1)} %get-tuple-element.66), channel_id=1, source_target_pairs={{0,2},{2,4},{4,6},{6,8},{8,10},{10,12},{12,14},{14,0},{1,3},{3,5},... | collective-permute-start | bytes 98312 | tf_op jit(solution)/shard_map/ppermute | solution.py:640
  30.5 4.9 %collective-permute-start.7 = (f32[4,16,128]{2,1,0:T(8,128)S(1)}, f32[4,16,128]{2,1,0:T(8,128)S(1)}, u32[]{:S(2)}, u32[]{:S(2)}) collective-permute-start(f32[4,16,128]{2,1,0:T(8,128)S(1)} %get-tuple-element.67), channel_id=1, source_target_pairs={{0,14},{2,0},{4,2},{6,4},{8,6},{10,8},{12,10},{14,12},{1,15},{3,1}... | collective-permute-start | bytes 98312 | tf_op jit(solution)/shard_map/ppermute | solution.py:640
  35.4 7.1 %collective-permute-start.9 = (f32[24,16,128]{2,1,0:T(8,128)S(1)}, f32[24,16,128]{2,1,0:T(8,128)S(1)}, u32[]{:S(2)}, u32[]{:S(2)}) collective-permute-start(f32[24,16,128]{2,1,0:T(8,128)S(1)} %constant_dynamic-update-slice_fusion.own), channel_id=1, source_target_pairs={{0,112},{16,0},{32,16},{48,32},{64,48},{80,64},{96,80},{112,96},{1... | collective-permute-start | bytes 589832 | tf_op jit(solution)/shard_map/ppermute | solution.py:640
  38.6 3.9 %collective-permute-start.8 = (f32[24,16,128]{2,1,0:T(8,128)S(1)}, f32[24,16,128]{2,1,0:T(8,128)S(1)}, u32[]{:S(2)}, u32[]{:S(2)}) collective-permute-start(f32[24,16,128]{2,1,0:T(8,128)S(1)} %constant_dynamic-update-slice_fusion.own), channel_id=1, source_target_pairs={{0,16},{16,32},{32,48},{48,64},{64,80},{80,96},{96,112},{112,0},{1... | collective-permute-start | bytes 589832 | tf_op jit(solution)/shard_map/ppermute | solution.py:640

commit v3 on v2

--- a/solution.py
+++ b/solution.py
@@ -23,10 +23,7 @@
     k_down0=2.0,
     k_coeff=2.0,
     k_down12=3.0,
-    k_whole=2.0,
-    k_up2=0.5,
-    k_up1=1.5,
-    k_up0=2.5,
+    k_up=6.0,
 )
 A0, B0, U0 = 12, 8, 3
 A1, U1 = 4, 8
@@ -635,6 +632,16 @@
         copy.wait()
 
 
+def k_up(
+    gathered, g2, c2, s2, q2, g1, c1, s1, q1, gm, cm, sm, q0, gw, cw, sw, qw, out,
+    u3, t3, x4, p3, u2, p2, u1, p1, va, vb, *rest,
+):
+    k_whole(gathered, u3, t3, x4, p3)
+    k_up2(u3, g2, c2, s2, q2, u2, p2)
+    k_up1(u2, g1, c1, s1, q1, u1, p1, va, vb)
+    k_up0(u1, gm, cm, sm, q0, gw, cw, sw, qw, out, *rest)
+
+
 def ring(v, axis, step):
     n = lax.axis_size(axis)
     return lax.ppermute(v, axis, [(i, (i + step) % n) for i in range(n)])
@@ -696,18 +703,14 @@
     )
     gathered = lax.all_to_all(chunk.reshape(64, 1, 1536), ("gx", "gy"), 0, 0, tiled=True)
     gathered = gathered.reshape(192, 4, 128)
-    (u3,) = run(
-        k_whole, (gathered,), [(8, 32, 128)], [(3, 8, 32, 128), (4, 32, 128), (4, 32, 128)]
-    )
-    (u2,) = run(k_up2, (u3, g2, c2, s2, q2), [(16, 24, 128)], [(8, 24, 128)])
-    (u1,) = run(
-        k_up1, (u2, g1, c1, s1, q1), [(34, 40, 128)], [(16, 40, 128)] + [(34, 40, 128)] * 2
-    )
     (out,) = run(
-        k_up0,
-        (u1, gm, cm, sm, q0, gw, cw, sw, qw),
+        k_up,
+        (gathered, g2, c2, s2, q2, g1, c1, s1, q1, gm, cm, sm, q0, gw, cw, sw, qw),
         [(32, 32, 128)],
-        [(18, 40, 128)] * 3 + [(38, 40, 128)] * 2 + small * 2 + [(32, 32, 128)],
+        [(8, 32, 128), (3, 8, 32, 128), (4, 32, 128), (4, 32, 128)]
+        + [(16, 24, 128), (8, 24, 128)]
+        + [(34, 40, 128), (16, 40, 128), (34, 40, 128), (34, 40, 128)]
+        + [(18, 40, 128)] * 3 + [(38, 40, 128)] * 2 + small * 2 + [(32, 32, 128)],
         HBM,
         [(32 // B0,)],
     )

time: 70.6 us -> 70.6 us (level)
    pallas_call x15 -> x12, Pallas kernels: 12.7 us -> 12.7 us  [run(): pl.pallas_call(body, out_shape=[jax.ShapeDtypeStruct(o, F32) for o in out...]
where the time goes in v3:
time: 70.6 us; the launch traced here: 70.3 us
  starting transfers between devices  29.5 us (42%)
  blocking collectives  19.7 us (28%)
  Pallas kernels  12.7 us (18%)
  waiting for transfers between devices  5.02 us (7%)
  local copies, waits for them, and re-layouts  2.11 us (3%)
  other arithmetic  0.99 us (1%)
    ppermute x15, starting transfers between devices, ring(): return lax.ppermute(v, axis, [(i, (i + step) % n) for i in range(n)])  29.5 us
    all_to_all x1, blocking collectives, shards(): lax.all_to_all(chunk.reshape(64, 1, 1536), ('gx', 'gy'), 0, 0, tiled=True)  19.7 us
    pallas_call x12, Pallas kernels, run(): pl.pallas_call(body, out_shape=[jax.ShapeDtypeStruct(o, F32) for o in out...  12.7 us
    ppermute x15, waiting for transfers between devices, ring(): return lax.ppermute(v, axis, [(i, (i + step) % n) for i in range(n)])  5.02 us
    unnamed x10, local copies, waits for them, and re-layouts  2.11 us
  transfers between devices with their start and end apart: 15, of which 4 were waited for; matrix products, arithmetic and copies ran while one was open for 0% of the time, Pallas kernels for 7%

profile of v3, /device:TPU:1, one launch (start us, length us, event | category | flops | bytes accessed | tf_op | source)
XLA Modules:
  0.0 70.3 jit_solution(773334160075765944)
XLA Ops:
  0.0 0.9 %compare_select_fusion.1 = (f32[3,32,128]{2,1,0:T(8,128)S(1)}, f32[3,32,128]{2,1,0:T(8,128)S(1)}, f32[3,32,128]{2,1,0:T(8,128)S(1)}) fusion(f32[32,32,128]{2,1,0:T(8,128)} %k.1, s32[]{:T(128)S(6)} %select_n.14, f32[32,32,128]{2,1,0:T(8,128)} %s.7, f32[32,32,128]{2,1,0:T(8,128)} %f.3), kind=kLoop, calls=%fused_computation.7 | loop fusion | flops 135168 | bytes 294916 | tf_op jit(solution)/shard_map/jit(_where)/select_n | solution.py:668
  1.0 3.7 %collective-permute-start = (f32[7,32,128]{2,1,0:T(8,128)S(1)}, f32[7,32,128]{2,1,0:T(8,128)S(1)}, u32[]{:S(2)}, u32[]{:S(2)}) collective-permute-start(f32[7,32,128]{2,1,0:T(8,128)S(1)} %shard_map.38), channel_id=1, source_target_pairs={{0,1},{1,0},{2,3},{3,2},{4,5},{5,4},{6,7},{7,6},{8,9},{9,8},{10,11... | collective-permute-start | bytes 344072 | tf_op jit(solution)/shard_map/ppermute | solution.py:647
  4.6 1.0 %copy-done.1 = f32[32,32,128]{2,1,0:T(8,128)S(1)} copy-done((f32[32,32,128]{2,1,0:T(8,128)S(1)}, f32[32,32,128]{2,1,0:T(8,128)}, u32[]{:S(2)}) %copy-start.1) | copy-done | bytes 524312
  5.7 1.0 %copy-done.3 = f32[32,32,128]{2,1,0:T(8,128)S(1)} copy-done((f32[32,32,128]{2,1,0:T(8,128)S(1)}, f32[32,32,128]{2,1,0:T(8,128)}, u32[]{:S(2)}) %copy-start.3) | copy-done | bytes 524312
  6.7 0.5 shard_map.37
  7.2 0.1 shard_map.39
  7.3 2.9 %collective-permute-start.1 = (f32[38,8,128]{2,1,0:T(8,128)S(1)}, f32[38,8,128]{2,1,0:T(8,128)S(1)}, u32[]{:S(2)}, u32[]{:S(2)}) collective-permute-start(f32[38,8,128]{2,1,0:T(8,128)S(1)} %get-tuple-element.51), channel_id=1, source_target_pairs={{0,16},{16,32},{32,48},{48,64},{64,80},{80,96},{96,112},{112,0},{1... | collective-permute-start | bytes 466952 | tf_op jit(solution)/shard_map/ppermute | solution.py:647
  10.2 2.7 %collective-permute-start.10 = (f32[16,16,128]{2,1,0:T(8,128)S(1)}, f32[16,16,128]{2,1,0:T(8,128)S(1)}, u32[]{:S(2)}, u32[]{:S(2)}) collective-permute-start(f32[16,16,128]{2,1,0:T(8,128)S(1)} %get-tuple-element.70), channel_id=1, source_target_pairs={{0,1},{1,0},{2,3},{3,2},{4,5},{5,4},{6,7},{7,6},{8,9},{9,8},{10,11... | collective-permute-start | bytes 393224 | tf_op jit(solution)/shard_map/ppermute | solution.py:647
  13.0 0.5 shard_map.41
  13.5 1.4 %collective-permute-done.2.from_right = f32[38,8,128]{2,1,0:T(8,128)S(1)} collective-permute-done((f32[38,8,128]{2,1,0:T(8,128)S(1)}, f32[38,8,128]{2,1,0:T(8,128)S(1)}, u32[]{:S(2)}, u32[]{:S(2)}) %collective-permute-start.2) | collective-permute-done | bytes 155680 | tf_op jit(solution)/shard_map/ppermute | solution.py:647
  14.9 0.3 shard_map.42
  15.2 1.3 %collective-permute-start.3 = (f32[3,40,128]{2,1,0:T(8,128)S(1)}, f32[3,40,128]{2,1,0:T(8,128)S(1)}, u32[]{:S(2)}, u32[]{:S(2)}) collective-permute-start(f32[3,40,128]{2,1,0:T(8,128)S(1)} %get-tuple-element.62), channel_id=1, source_target_pairs={{0,2},{2,4},{4,6},{6,8},{8,10},{10,12},{12,14},{14,0},{1,3},{3,5},... | collective-permute-start | bytes 184328 | tf_op jit(solution)/shard_map/ppermute | solution.py:647
  16.5 3.6 %collective-permute-start.4 = (f32[3,40,128]{2,1,0:T(8,128)S(1)}, f32[3,40,128]{2,1,0:T(8,128)S(1)}, u32[]{:S(2)}, u32[]{:S(2)}) collective-permute-start(f32[3,40,128]{2,1,0:T(8,128)S(1)} %get-tuple-element.63), channel_id=1, source_target_pairs={{0,14},{2,0},{4,2},{6,4},{8,6},{10,8},{12,10},{14,12},{1,15},{3,1}... | collective-permute-start | bytes 184328 | tf_op jit(solution)/shard_map/ppermute | solution.py:647
  20.1 0.2 shard_map.40
  20.3 0.2 shard_map.45
  20.5 0.1 collective-permute-start.11
  20.6 3.6 %collective-permute-start.12 = (f32[7,16,128]{2,1,0:T(8,128)S(1)}, f32[7,16,128]{2,1,0:T(8,128)S(1)}, u32[]{:S(2)}, u32[]{:S(2)}) collective-permute-start(f32[7,16,128]{2,1,0:T(8,128)S(1)} %get-tuple-element.74), channel_id=1, source_target_pairs={{0,14},{2,0},{4,2},{6,4},{8,6},{10,8},{12,10},{14,12},{1,15},{3,1}... | collective-permute-start | bytes 172040 | tf_op jit(solution)/shard_map/ppermute | solution.py:647
  24.2 1.4 %shard_map.43 = (f32[6,40,128]{2,1,0:T(8,128)S(1)}, f32[6,40,128]{2,1,0:T(8,128)S(1)}, f32[6,40,128]{2,1,0:T(8,128)S(1)}, f32[38,40,128]{2,1,0:T(8,128)S(1)}, f3...) custom-call(f32[32,32,128]{2,1,0:T(8,128)S(1)} %copy-done.2, f32[38,40,128]{2,1,0:T(8,128)S(1)} %get-tuple-element.53.gm, ...), custom_call_target="tpu_custom_call" | custom-call | bytes 7000000 | tf_op jit(solution)/shard_map/pallas_call | solution.py:34
  25.6 2.5 %collective-permute-start.5 = (f32[8,16,128]{2,1,0:T(8,128)S(1)}, f32[8,16,128]{2,1,0:T(8,128)S(1)}, u32[]{:S(2)}, u32[]{:S(2)}) collective-permute-start(f32[8,16,128]{2,1,0:T(8,128)S(1)} %get-tuple-element.64), channel_id=1, source_target_pairs={{0,1},{1,0},{2,3},{3,2},{4,5},{5,4},{6,7},{7,6},{8,9},{9,8},{10,11... | collective-permute-start | bytes 196616 | tf_op jit(solution)/shard_map/ppermute | solution.py:647
  28.2 1.2 %collective-permute-start.14 = (f32[46,16,128]{2,1,0:T(8,128)S(1)}, f32[46,16,128]{2,1,0:T(8,128)S(1)}, u32[]{:S(2)}, u32[]{:S(2)}) collective-permute-start(f32[46,16,128]{2,1,0:T(8,128)S(1)} %pad_maximum_fusion.own), channel_id=1, source_target_pairs={{0,112},{16,0},{32,16},{48,32},{64,48},{80,64},{96,80},{112,96},{1... | collective-permute-start | bytes 1130504 | tf_op jit(solution)/shard_map/ppermute | solution.py:647
  29.3 0.6 collective-permute-start.13
  29.9 0.4 collective-permute-done.5
  30.3 0.1 shard_map.44
  30.5 3.6 %collective-permute-start.7 = (f32[4,16,128]{2,1,0:T(8,128)S(1)}, f32[4,16,128]{2,1,0:T(8,128)S(1)}, u32[]{:S(2)}, u32[]{:S(2)}) collective-permute-start(f32[4,16,128]{2,1,0:T(8,128)S(1)} %get-tuple-element.67), channel_id=1, source_target_pairs={{0,14},{2,0},{4,2},{6,4},{8,6},{10,8},{12,10},{14,12},{1,15},{3,1}... | collective-permute-start | bytes 98312 | tf_op jit(solution)/shard_map/ppermute | solution.py:647
  34.1 1.3 %collective-permute-done.6 = f32[4,16,128]{2,1,0:T(8,128)S(1)} collective-permute-done((f32[4,16,128]{2,1,0:T(8,128)S(1)}, f32[4,16,128]{2,1,0:T(8,128)S(1)}, u32[]{:S(2)}, u32[]{:S(2)}) %collective-permute-start.6) | collective-permute-done | bytes 32800 | tf_op jit(solution)/shard_map/ppermute | solution.py:647
  35.4 3.2 %collective-permute-start.9 = (f32[24,16,128]{2,1,0:T(8,128)S(1)}, f32[24,16,128]{2,1,0:T(8,128)S(1)}, u32[]{:S(2)}, u32[]{:S(2)}) collective-permute-start(f32[24,16,128]{2,1,0:T(8,128)S(1)} %constant_dynamic-update-slice_fusion.own), channel_id=1, source_target_pairs={{0,112},{16,0},{32,16},{48,32},{64,48},{80,64},{96,80},{112,96},{1... | collective-permute-start | bytes 589832 | tf_op jit(solution)/shard_map/ppermute | solution.py:647
  38.6 0.6 collective-permute-start.8
  39.2 1.3 %shard_map.46 = (f32[32,40,128]{2,1,0:T(8,128)S(1)}, f32[32,40,128]{2,1,0:T(8,128)S(1)}, f32[32,40,128]{2,1,0:T(8,128)S(1)}, f32[16,24,128]{2,1,0:T(8,128)S(1)},...) custom-call(f32[46,16,128]{2,1,0:T(8,128)S(1)} %pad_maximum_fusion.own, ...), custom_call_target="tpu_custom_call" | custom-call | bytes 7000000 | tf_op jit(solution)/shard_map/pallas_call | solution.py:34
  40.5 2.0 %collective-permute-done.9.xr = f32[24,16,128]{2,1,0:T(8,128)S(1)} collective-permute-done((f32[24,16,128]{2,1,0:T(8,128)S(1)}, f32[24,16,128]{2,1,0:T(8,128)S(1)}, u32[]{:S(2)}, u32[]{:S(2)}) %collective-permute-start.9) | collective-permute-done | bytes 196640 | tf_op jit(solution)/shard_map/ppermute | solution.py:647
  42.5 2.1 %shard_map.47 = (f32[34,40,128]{2,1,0:T(8,128)S(1)}, f32[34,40,128]{2,1,0:T(8,128)S(1)}, f32[16,24,128]{2,1,0:T(8,128)S(1)}, f32[16,24,128]{2,1,0:T(8,128)S(1)}, f32[96,8,128]{2,1,0:T(8,128)S(1)}) custom-call(f32[24,16,128]{2,1,0:T(8,128)S(1)} %constant_dynamic-update-slice_fusion.own, f32[24,16,128]{2,1,0:T(8,128)S(1)} %collective-permute-done.8.xl, ...), custom_call_target="tpu_custom_call" | custom-call | bytes 10500000 | tf_op jit(solution)/shard_map/pallas_call | solution.py:34
  44.6 19.7 %all_to_all.5 = f32[64,1,1536]{2,1,0:T(1,128)S(1)} all-to-all(f32[64,1,1536]{2,1,0:T(1,128)S(1)} %bitcast.3), channel_id=1, replica_groups=mesh['gx'=8,'gy'=8,'gz'=2] {'gx','gy'}, dimensions={0} | all-to-all | bytes 786432 | tf_op jit(solution)/shard_map/all_to_all | solution.py:704
  64.4 5.8 %shard_map.48 = f32[32,32,128]{2,1,0:T(8,128)} custom-call(f32[192,4,128]{2,1,0:T(4,128)S(1)} %bitcast.2, f32[16,24,128]{2,1,0:T(8,128)S(1)} %get-tuple-element.84.g2, f32[16,24,128]{2,1,0:T(8,128)S(1)} %get-tuple-element.80.c2, f32[16,24,128]{2,1,0:T(8,128)S(1)} %get-tuple-element.79.s2, f32[16,24,128]{2,1,0:T(8,128)S(1)} %get-tuple-element.85.q2, ...), custom_call_target="tpu_custom_call" | custom-call | bytes 21000000 | tf_op jit(solution)/shard_map/pallas_call | solution.py:34
  (26 shorter events, 0.2 us)
Async XLA Ops:
  0.0 4.6 %copy-start = (f32[32,32,128]{2,1,0:T(8,128)S(1)}, f32[32,32,128]{2,1,0:T(8,128)}, u32[]{:S(2)}) copy-start(f32[32,32,128]{2,1,0:T(8,128)} %s.7) | copy-start | bytes 1572868
  1.0 6.2 %collective-permute-start = (f32[7,32,128]{2,1,0:T(8,128)S(1)}, f32[7,32,128]{2,1,0:T(8,128)S(1)}, u32[]{:S(2)}, u32[]{:S(2)}) collective-permute-start(f32[7,32,128]{2,1,0:T(8,128)S(1)} %shard_map.38), channel_id=1, source_target_pairs={{0,1},{1,0},{2,3},{3,2},{4,5},{5,4},{6,7},{7,6},{8,9},{9,8},{10,11... | collective-permute-start | bytes 344072 | tf_op jit(solution)/shard_map/ppermute | solution.py:647
  4.6 1.0 %copy-start.1 = (f32[32,32,128]{2,1,0:T(8,128)S(1)}, f32[32,32,128]{2,1,0:T(8,128)}, u32[]{:S(2)}) copy-start(f32[32,32,128]{2,1,0:T(8,128)} %f.3) | copy-start | bytes 1572868
  5.7 1.0 %copy-start.3 = (f32[32,32,128]{2,1,0:T(8,128)S(1)}, f32[32,32,128]{2,1,0:T(8,128)}, u32[]{:S(2)}) copy-start(f32[32,32,128]{2,1,0:T(8,128)} %k.1) | copy-start | bytes 1572868
  7.3 6.2 %collective-permute-start.1 = (f32[38,8,128]{2,1,0:T(8,128)S(1)}, f32[38,8,128]{2,1,0:T(8,128)S(1)}, u32[]{:S(2)}, u32[]{:S(2)}) collective-permute-start(f32[38,8,128]{2,1,0:T(8,128)S(1)} %get-tuple-element.51), channel_id=1, source_target_pairs={{0,16},{16,32},{32,48},{48,64},{64,80},{80,96},{96,112},{112,0},{1... | collective-permute-start | bytes 466952 | tf_op jit(solution)/shard_map/ppermute | solution.py:647
  10.2 4.7 %collective-permute-start.2 = (f32[38,8,128]{2,1,0:T(8,128)S(1)}, f32[38,8,128]{2,1,0:T(8,128)S(1)}, u32[]{:S(2)}, u32[]{:S(2)}) collective-permute-start(f32[38,8,128]{2,1,0:T(8,128)S(1)} %get-tuple-element.52), channel_id=1, source_target_pairs={{0,112},{16,0},{32,16},{48,32},{64,48},{80,64},{96,80},{112,96},{1... | collective-permute-start | bytes 466952 | tf_op jit(solution)/shard_map/ppermute | solution.py:647
  10.2 10.0 %collective-permute-start.10 = (f32[16,16,128]{2,1,0:T(8,128)S(1)}, f32[16,16,128]{2,1,0:T(8,128)S(1)}, u32[]{:S(2)}, u32[]{:S(2)}) collective-permute-start(f32[16,16,128]{2,1,0:T(8,128)S(1)} %get-tuple-element.70), channel_id=1, source_target_pairs={{0,1},{1,0},{2,3},{3,2},{4,5},{5,4},{6,7},{7,6},{8,9},{9,8},{10,11... | collective-permute-start | bytes 393224 | tf_op jit(solution)/shard_map/ppermute | solution.py:647
  15.2 8.9 %collective-permute-start.3 = (f32[3,40,128]{2,1,0:T(8,128)S(1)}, f32[3,40,128]{2,1,0:T(8,128)S(1)}, u32[]{:S(2)}, u32[]{:S(2)}) collective-permute-start(f32[3,40,128]{2,1,0:T(8,128)S(1)} %get-tuple-element.62), channel_id=1, source_target_pairs={{0,2},{2,4},{4,6},{6,8},{8,10},{10,12},{12,14},{14,0},{1,3},{3,5},... | collective-permute-start | bytes 184328 | tf_op jit(solution)/shard_map/ppermute | solution.py:647
  16.5 7.6 %collective-permute-start.4 = (f32[3,40,128]{2,1,0:T(8,128)S(1)}, f32[3,40,128]{2,1,0:T(8,128)S(1)}, u32[]{:S(2)}, u32[]{:S(2)}) collective-permute-start(f32[3,40,128]{2,1,0:T(8,128)S(1)} %get-tuple-element.63), channel_id=1, source_target_pairs={{0,14},{2,0},{4,2},{6,4},{8,6},{10,8},{12,10},{14,12},{1,15},{3,1}... | collective-permute-start | bytes 184328 | tf_op jit(solution)/shard_map/ppermute | solution.py:647
  20.2 3.9 %copy-start.2 = (f32[32,32,128]{2,1,0:T(8,128)S(1)}, f32[32,32,128]{2,1,0:T(8,128)}, u32[]{:S(2)}) copy-start(f32[32,32,128]{2,1,0:T(8,128)} %f.3) | copy-start | bytes 1572868
  20.5 7.6 %collective-permute-start.11 = (f32[7,16,128]{2,1,0:T(8,128)S(1)}, f32[7,16,128]{2,1,0:T(8,128)S(1)}, u32[]{:S(2)}, u32[]{:S(2)}) collective-permute-start(f32[7,16,128]{2,1,0:T(8,128)S(1)} %get-tuple-element.73), channel_id=1, source_target_pairs={{0,2},{2,4},{4,6},{6,8},{8,10},{10,12},{12,14},{14,0},{1,3},{3,5},... | collective-permute-start | bytes 172040 | tf_op jit(solution)/shard_map/ppermute | solution.py:647
  20.6 7.5 %collective-permute-start.12 = (f32[7,16,128]{2,1,0:T(8,128)S(1)}, f32[7,16,128]{2,1,0:T(8,128)S(1)}, u32[]{:S(2)}, u32[]{:S(2)}) collective-permute-start(f32[7,16,128]{2,1,0:T(8,128)S(1)} %get-tuple-element.74), channel_id=1, source_target_pairs={{0,14},{2,0},{4,2},{6,4},{8,6},{10,8},{12,10},{14,12},{1,15},{3,1}... | collective-permute-start | bytes 172040 | tf_op jit(solution)/shard_map/ppermute | solution.py:647
  25.6 4.7 %collective-permute-start.5 = (f32[8,16,128]{2,1,0:T(8,128)S(1)}, f32[8,16,128]{2,1,0:T(8,128)S(1)}, u32[]{:S(2)}, u32[]{:S(2)}) collective-permute-start(f32[8,16,128]{2,1,0:T(8,128)S(1)} %get-tuple-element.64), channel_id=1, source_target_pairs={{0,1},{1,0},{2,3},{3,2},{4,5},{5,4},{6,7},{7,6},{8,9},{9,8},{10,11... | collective-permute-start | bytes 196616 | tf_op jit(solution)/shard_map/ppermute | solution.py:647
  28.2 11.0 %collective-permute-start.14 = (f32[46,16,128]{2,1,0:T(8,128)S(1)}, f32[46,16,128]{2,1,0:T(8,128)S(1)}, u32[]{:S(2)}, u32[]{:S(2)}) collective-permute-start(f32[46,16,128]{2,1,0:T(8,128)S(1)} %pad_maximum_fusion.own), channel_id=1, source_target_pairs={{0,112},{16,0},{32,16},{48,32},{64,48},{80,64},{96,80},{112,96},{1... | collective-permute-start | bytes 1130504 | tf_op jit(solution)/shard_map/ppermute | solution.py:647
  29.3 9.8 %collective-permute-start.13 = (f32[46,16,128]{2,1,0:T(8,128)S(1)}, f32[46,16,128]{2,1,0:T(8,128)S(1)}, u32[]{:S(2)}, u32[]{:S(2)}) collective-permute-start(f32[46,16,128]{2,1,0:T(8,128)S(1)} %pad_maximum_fusion.own), channel_id=1, source_target_pairs={{0,16},{16,32},{32,48},{48,64},{64,80},{80,96},{96,112},{112,0},{1... | collective-permute-start | bytes 1130504 | tf_op jit(solution)/shard_map/ppermute | solution.py:647
  30.4 4.9 %collective-permute-start.6 = (f32[4,16,128]{2,1,0:T(8,128)S(1)}, f32[4,16,128]{2,1,0:T(8,128)S(1)}, u32[]{:S(2)}, u32[]{:S(2)}) collective-permute-start(f32[4,16,128]{2,1,0:T(8,128)S(1)} %get-tuple-element.66), channel_id=1, source_target_pairs={{0,2},{2,4},{4,6},{6,8},{8,10},{10,12},{12,14},{14,0},{1,3},{3,5},... | collective-permute-start | bytes 98312 | tf_op jit(solution)/shard_map/ppermute | solution.py:647
  30.5 4.9 %collective-permute-start.7 = (f32[4,16,128]{2,1,0:T(8,128)S(1)}, f32[4,16,128]{2,1,0:T(8,128)S(1)}, u32[]{:S(2)}, u32[]{:S(2)}) collective-permute-start(f32[4,16,128]{2,1,0:T(8,128)S(1)} %get-tuple-element.67), channel_id=1, source_target_pairs={{0,14},{2,0},{4,2},{6,4},{8,6},{10,8},{12,10},{14,12},{1,15},{3,1}... | collective-permute-start | bytes 98312 | tf_op jit(solution)/shard_map/ppermute | solution.py:647
  35.4 7.1 %collective-permute-start.9 = (f32[24,16,128]{2,1,0:T(8,128)S(1)}, f32[24,16,128]{2,1,0:T(8,128)S(1)}, u32[]{:S(2)}, u32[]{:S(2)}) collective-permute-start(f32[24,16,128]{2,1,0:T(8,128)S(1)} %constant_dynamic-update-slice_fusion.own), channel_id=1, source_target_pairs={{0,112},{16,0},{32,16},{48,32},{64,48},{80,64},{96,80},{112,96},{1... | collective-permute-start | bytes 589832 | tf_op jit(solution)/shard_map/ppermute | solution.py:647
  38.6 3.9 %collective-permute-start.8 = (f32[24,16,128]{2,1,0:T(8,128)S(1)}, f32[24,16,128]{2,1,0:T(8,128)S(1)}, u32[]{:S(2)}, u32[]{:S(2)}) collective-permute-start(f32[24,16,128]{2,1,0:T(8,128)S(1)} %constant_dynamic-update-slice_fusion.own), channel_id=1, source_target_pairs={{0,16},{16,32},{32,48},{48,64},{64,80},{80,96},{96,112},{112,0},{1... | collective-permute-start | bytes 589832 | tf_op jit(solution)/shard_map/ppermute | solution.py:647

commit v4 on v2

--- a/solution.py
+++ b/solution.py
@@ -30,6 +30,7 @@
 )
 A0, B0, U0 = 12, 8, 3
 A1, U1 = 4, 8
+PARTS = ((0, 8), (8, 8), (16, 8), (24, 4), (28, 4))
 
 
 def run(body, args, outs, scratch=(), out_spec=VM, sems=()):
@@ -622,12 +623,12 @@
     blocks(1, 36, A0, sweep, U0)
 
     copies = []
-    for b in range(32 // B0):
-        z = 3 + b * B0
-        at = pl.ds(z, B0)
-        n = near_main(wb, eb, z, B0)[:, :32]
+    for b, (first, size) in enumerate(PARTS):
+        z = 3 + first
+        at = pl.ds(z, size)
+        n = near_main(wb, eb, z, size)[:, :32]
         v = (0.2 * wb[at, :32, :] + gm[at, :32, :]) + cm[at, :32, :] * n
-        part = pl.ds(z - 3, B0)
+        part = pl.ds(first, size)
         done[part] = v / sm[at, :32, :]
         copies.append(pltpu.make_async_copy(done.at[part], out.at[part], sem.at[b]))
         copies[-1].start()
@@ -709,7 +710,7 @@
         [(32, 32, 128)],
         [(18, 40, 128)] * 3 + [(38, 40, 128)] * 2 + small * 2 + [(32, 32, 128)],
         HBM,
-        [(32 // B0,)],
+        [(len(PARTS),)],
     )
     return out
 

time: 70.6 us -> 70.6 us (level)
  no operation moved by 1% of the time
where the time goes in v4:
time: 70.6 us; the launch traced here: 70.4 us
  starting transfers between devices  29.5 us (42%)
  blocking collectives  19.7 us (28%)
  Pallas kernels  12.7 us (18%)
  waiting for transfers between devices  5.02 us (7%)
  local copies, waits for them, and re-layouts  2.11 us (3%)
  other arithmetic  0.98 us (1%)
    ppermute x15, starting transfers between devices, ring(): return lax.ppermute(v, axis, [(i, (i + step) % n) for i in range(n)])  29.5 us
    all_to_all x1, blocking collectives, shards(): lax.all_to_all(chunk.reshape(64, 1, 1536), ('gx', 'gy'), 0, 0, tiled=True)  19.7 us
    pallas_call x15, Pallas kernels, run(): pl.pallas_call(body, out_shape=[jax.ShapeDtypeStruct(o, F32) for o in out...  12.7 us
    ppermute x15, waiting for transfers between devices, ring(): return lax.ppermute(v, axis, [(i, (i + step) % n) for i in range(n)])  5.02 us
    unnamed x10, local copies, waits for them, and re-layouts  2.11 us
  transfers between devices with their start and end apart: 15, of which 4 were waited for; matrix products, arithmetic and copies ran while one was open for 0% of the time, Pallas kernels for 7%

profile of v4, /device:TPU:1, one launch (start us, length us, event | category | flops | bytes accessed | tf_op | source)
XLA Modules:
  0.0 70.4 jit_solution(7509235346592534577)
XLA Ops:
  0.0 0.9 %compare_select_fusion.1 = (f32[3,32,128]{2,1,0:T(8,128)S(1)}, f32[3,32,128]{2,1,0:T(8,128)S(1)}, f32[3,32,128]{2,1,0:T(8,128)S(1)}) fusion(f32[32,32,128]{2,1,0:T(8,128)} %k.1, s32[]{:T(128)S(6)} %select_n.14, f32[32,32,128]{2,1,0:T(8,128)} %s.7, f32[32,32,128]{2,1,0:T(8,128)} %f.3), kind=kLoop, calls=%fused_computation.7 | loop fusion | flops 135168 | bytes 294916 | tf_op jit(solution)/shard_map/jit(_where)/select_n | solution.py:662
  1.0 3.7 %collective-permute-start = (f32[7,32,128]{2,1,0:T(8,128)S(1)}, f32[7,32,128]{2,1,0:T(8,128)S(1)}, u32[]{:S(2)}, u32[]{:S(2)}) collective-permute-start(f32[7,32,128]{2,1,0:T(8,128)S(1)} %shard_map.38), channel_id=1, source_target_pairs={{0,1},{1,0},{2,3},{3,2},{4,5},{5,4},{6,7},{7,6},{8,9},{9,8},{10,11... | collective-permute-start | bytes 344072 | tf_op jit(solution)/shard_map/ppermute | solution.py:641
  4.6 1.0 %copy-done.1 = f32[32,32,128]{2,1,0:T(8,128)S(1)} copy-done((f32[32,32,128]{2,1,0:T(8,128)S(1)}, f32[32,32,128]{2,1,0:T(8,128)}, u32[]{:S(2)}) %copy-start.1) | copy-done | bytes 524312
  5.7 1.0 %copy-done.3 = f32[32,32,128]{2,1,0:T(8,128)S(1)} copy-done((f32[32,32,128]{2,1,0:T(8,128)S(1)}, f32[32,32,128]{2,1,0:T(8,128)}, u32[]{:S(2)}) %copy-start.3) | copy-done | bytes 524312
  6.7 0.5 shard_map.37
  7.3 2.9 %collective-permute-start.1 = (f32[38,8,128]{2,1,0:T(8,128)S(1)}, f32[38,8,128]{2,1,0:T(8,128)S(1)}, u32[]{:S(2)}, u32[]{:S(2)}) collective-permute-start(f32[38,8,128]{2,1,0:T(8,128)S(1)} %get-tuple-element.51), channel_id=1, source_target_pairs={{0,16},{16,32},{32,48},{48,64},{64,80},{80,96},{96,112},{112,0},{1... | collective-permute-start | bytes 466952 | tf_op jit(solution)/shard_map/ppermute | solution.py:641
  10.2 2.7 %collective-permute-start.10 = (f32[16,16,128]{2,1,0:T(8,128)S(1)}, f32[16,16,128]{2,1,0:T(8,128)S(1)}, u32[]{:S(2)}, u32[]{:S(2)}) collective-permute-start(f32[16,16,128]{2,1,0:T(8,128)S(1)} %get-tuple-element.70), channel_id=1, source_target_pairs={{0,1},{1,0},{2,3},{3,2},{4,5},{5,4},{6,7},{7,6},{8,9},{9,8},{10,11... | collective-permute-start | bytes 393224 | tf_op jit(solution)/shard_map/ppermute | solution.py:641
  13.0 0.5 shard_map.41
  13.5 1.4 %collective-permute-done.2.from_right = f32[38,8,128]{2,1,0:T(8,128)S(1)} collective-permute-done((f32[38,8,128]{2,1,0:T(8,128)S(1)}, f32[38,8,128]{2,1,0:T(8,128)S(1)}, u32[]{:S(2)}, u32[]{:S(2)}) %collective-permute-start.2) | collective-permute-done | bytes 155680 | tf_op jit(solution)/shard_map/ppermute | solution.py:641
  14.9 0.3 shard_map.42
  15.2 1.3 %collective-permute-start.3 = (f32[3,40,128]{2,1,0:T(8,128)S(1)}, f32[3,40,128]{2,1,0:T(8,128)S(1)}, u32[]{:S(2)}, u32[]{:S(2)}) collective-permute-start(f32[3,40,128]{2,1,0:T(8,128)S(1)} %get-tuple-element.62), channel_id=1, source_target_pairs={{0,2},{2,4},{4,6},{6,8},{8,10},{10,12},{12,14},{14,0},{1,3},{3,5},... | collective-permute-start | bytes 184328 | tf_op jit(solution)/shard_map/ppermute | solution.py:641
  16.5 3.6 %collective-permute-start.4 = (f32[3,40,128]{2,1,0:T(8,128)S(1)}, f32[3,40,128]{2,1,0:T(8,128)S(1)}, u32[]{:S(2)}, u32[]{:S(2)}) collective-permute-start(f32[3,40,128]{2,1,0:T(8,128)S(1)} %get-tuple-element.63), channel_id=1, source_target_pairs={{0,14},{2,0},{4,2},{6,4},{8,6},{10,8},{12,10},{14,12},{1,15},{3,1}... | collective-permute-start | bytes 184328 | tf_op jit(solution)/shard_map/ppermute | solution.py:641
  20.1 0.2 shard_map.40
  20.3 0.2 shard_map.45
  20.6 3.6 %collective-permute-start.12 = (f32[7,16,128]{2,1,0:T(8,128)S(1)}, f32[7,16,128]{2,1,0:T(8,128)S(1)}, u32[]{:S(2)}, u32[]{:S(2)}) collective-permute-start(f32[7,16,128]{2,1,0:T(8,128)S(1)} %get-tuple-element.74), channel_id=1, source_target_pairs={{0,14},{2,0},{4,2},{6,4},{8,6},{10,8},{12,10},{14,12},{1,15},{3,1}... | collective-permute-start | bytes 172040 | tf_op jit(solution)/shard_map/ppermute | solution.py:641
  24.2 1.4 %shard_map.43 = (f32[6,40,128]{2,1,0:T(8,128)S(1)}, f32[6,40,128]{2,1,0:T(8,128)S(1)}, f32[6,40,128]{2,1,0:T(8,128)S(1)}, f32[38,40,128]{2,1,0:T(8,128)S(1)}, f3...) custom-call(f32[32,32,128]{2,1,0:T(8,128)S(1)} %copy-done.2, f32[38,40,128]{2,1,0:T(8,128)S(1)} %get-tuple-element.53.gm, ...), custom_call_target="tpu_custom_call" | custom-call | bytes 7000000 | tf_op jit(solution)/shard_map/pallas_call | solution.py:38
  25.6 2.5 %collective-permute-start.5 = (f32[8,16,128]{2,1,0:T(8,128)S(1)}, f32[8,16,128]{2,1,0:T(8,128)S(1)}, u32[]{:S(2)}, u32[]{:S(2)}) collective-permute-start(f32[8,16,128]{2,1,0:T(8,128)S(1)} %get-tuple-element.64), channel_id=1, source_target_pairs={{0,1},{1,0},{2,3},{3,2},{4,5},{5,4},{6,7},{7,6},{8,9},{9,8},{10,11... | collective-permute-start | bytes 196616 | tf_op jit(solution)/shard_map/ppermute | solution.py:641
  28.2 1.2 %collective-permute-start.14 = (f32[46,16,128]{2,1,0:T(8,128)S(1)}, f32[46,16,128]{2,1,0:T(8,128)S(1)}, u32[]{:S(2)}, u32[]{:S(2)}) collective-permute-start(f32[46,16,128]{2,1,0:T(8,128)S(1)} %pad_maximum_fusion.own), channel_id=1, source_target_pairs={{0,112},{16,0},{32,16},{48,32},{64,48},{80,64},{96,80},{112,96},{1... | collective-permute-start | bytes 1130504 | tf_op jit(solution)/shard_map/ppermute | solution.py:641
  29.3 0.6 collective-permute-start.13
  29.9 0.4 collective-permute-done.5
  30.5 3.6 %collective-permute-start.7 = (f32[4,16,128]{2,1,0:T(8,128)S(1)}, f32[4,16,128]{2,1,0:T(8,128)S(1)}, u32[]{:S(2)}, u32[]{:S(2)}) collective-permute-start(f32[4,16,128]{2,1,0:T(8,128)S(1)} %get-tuple-element.67), channel_id=1, source_target_pairs={{0,14},{2,0},{4,2},{6,4},{8,6},{10,8},{12,10},{14,12},{1,15},{3,1}... | collective-permute-start | bytes 98312 | tf_op jit(solution)/shard_map/ppermute | solution.py:641
  34.1 1.3 %collective-permute-done.6 = f32[4,16,128]{2,1,0:T(8,128)S(1)} collective-permute-done((f32[4,16,128]{2,1,0:T(8,128)S(1)}, f32[4,16,128]{2,1,0:T(8,128)S(1)}, u32[]{:S(2)}, u32[]{:S(2)}) %collective-permute-start.6) | collective-permute-done | bytes 32800 | tf_op jit(solution)/shard_map/ppermute | solution.py:641
  35.4 3.2 %collective-permute-start.9 = (f32[24,16,128]{2,1,0:T(8,128)S(1)}, f32[24,16,128]{2,1,0:T(8,128)S(1)}, u32[]{:S(2)}, u32[]{:S(2)}) collective-permute-start(f32[24,16,128]{2,1,0:T(8,128)S(1)} %constant_dynamic-update-slice_fusion.own), channel_id=1, source_target_pairs={{0,112},{16,0},{32,16},{48,32},{64,48},{80,64},{96,80},{112,96},{1... | collective-permute-start | bytes 589832 | tf_op jit(solution)/shard_map/ppermute | solution.py:641
  38.6 0.6 collective-permute-start.8
  39.2 1.3 %shard_map.46 = (f32[32,40,128]{2,1,0:T(8,128)S(1)}, f32[32,40,128]{2,1,0:T(8,128)S(1)}, f32[32,40,128]{2,1,0:T(8,128)S(1)}, f32[16,24,128]{2,1,0:T(8,128)S(1)},...) custom-call(f32[46,16,128]{2,1,0:T(8,128)S(1)} %pad_maximum_fusion.own, ...), custom_call_target="tpu_custom_call" | custom-call | bytes 7000000 | tf_op jit(solution)/shard_map/pallas_call | solution.py:38
  40.5 2.0 %collective-permute-done.9.xr = f32[24,16,128]{2,1,0:T(8,128)S(1)} collective-permute-done((f32[24,16,128]{2,1,0:T(8,128)S(1)}, f32[24,16,128]{2,1,0:T(8,128)S(1)}, u32[]{:S(2)}, u32[]{:S(2)}) %collective-permute-start.9) | collective-permute-done | bytes 196640 | tf_op jit(solution)/shard_map/ppermute | solution.py:641
  42.5 2.1 %shard_map.47 = (f32[34,40,128]{2,1,0:T(8,128)S(1)}, f32[34,40,128]{2,1,0:T(8,128)S(1)}, f32[16,24,128]{2,1,0:T(8,128)S(1)}, f32[16,24,128]{2,1,0:T(8,128)S(1)}, f32[96,8,128]{2,1,0:T(8,128)S(1)}) custom-call(f32[24,16,128]{2,1,0:T(8,128)S(1)} %constant_dynamic-update-slice_fusion.own, f32[24,16,128]{2,1,0:T(8,128)S(1)} %collective-permute-done.8.xl, ...), custom_call_target="tpu_custom_call" | custom-call | bytes 10500000 | tf_op jit(solution)/shard_map/pallas_call | solution.py:38
  44.6 19.7 %all_to_all.5 = f32[64,1,1536]{2,1,0:T(1,128)S(1)} all-to-all(f32[64,1,1536]{2,1,0:T(1,128)S(1)} %bitcast.3), channel_id=1, replica_groups=mesh['gx'=8,'gy'=8,'gz'=2] {'gx','gy'}, dimensions={0} | all-to-all | bytes 786432 | tf_op jit(solution)/shard_map/all_to_all | solution.py:698
  64.4 1.9 %shard_map.48.u3 = f32[8,32,128]{2,1,0:T(8,128)S(1)} custom-call(f32[192,4,128]{2,1,0:T(4,128)S(1)} %bitcast.2), custom_call_target="tpu_custom_call" | custom-call | bytes 7000000 | tf_op jit(solution)/shard_map/pallas_call | solution.py:38
  66.2 0.5 shard_map.49.u2
  66.8 1.0 %shard_map.50.u1 = f32[34,40,128]{2,1,0:T(8,128)S(1)} custom-call(f32[16,24,128]{2,1,0:T(8,128)S(1)} %shard_map.49.u2, f32[34,40,128]{2,1,0:T(8,128)S(1)} %get-tuple-element.86.g1, f32[32,40,128]{2,1,0:T(8,128)S(1)} %get-tuple-element.77.c1, f32[32,40,128]{2,1,0:T(8,128)S(1)} %get-tuple-element.76.s1, f32[34,40,128]{2,1,0:T(8,128)S(1)} %get-tuple-element.87.q1), custom_call_target="tpu_custom_call" | custom-call | bytes 5250000 | tf_op jit(solution)/shard_map/pallas_call | solution.py:38
  67.8 2.4 %shard_map.51 = f32[32,32,128]{2,1,0:T(8,128)} custom-call(f32[34,40,128]{2,1,0:T(8,128)S(1)} %shard_map.50.u1, f32[38,40,128]{2,1,0:T(8,128)S(1)} %get-tuple-element.53.gm, f32[38,40,128]{2,1,0:T(8,128)S(1)} %get-tuple-element.54.cm, f32[38,40,128]{2,1,0:T(8,128)S(1)} %get-tuple-element.55.sm, f32[38,40,128]{2,1,0:T(8,128)S(1)} %get-tuple-element.88.q, ...), custom_call_target="tpu_custom_call" | custom-call | bytes 8750000 | tf_op jit(solution)/shard_map/pallas_call | solution.py:38
  (29 shorter events, 0.5 us)
Async XLA Ops:
  0.0 4.6 %copy-start = (f32[32,32,128]{2,1,0:T(8,128)S(1)}, f32[32,32,128]{2,1,0:T(8,128)}, u32[]{:S(2)}) copy-start(f32[32,32,128]{2,1,0:T(8,128)} %s.7) | copy-start | bytes 1572868
  1.0 6.2 %collective-permute-start = (f32[7,32,128]{2,1,0:T(8,128)S(1)}, f32[7,32,128]{2,1,0:T(8,128)S(1)}, u32[]{:S(2)}, u32[]{:S(2)}) collective-permute-start(f32[7,32,128]{2,1,0:T(8,128)S(1)} %shard_map.38), channel_id=1, source_target_pairs={{0,1},{1,0},{2,3},{3,2},{4,5},{5,4},{6,7},{7,6},{8,9},{9,8},{10,11... | collective-permute-start | bytes 344072 | tf_op jit(solution)/shard_map/ppermute | solution.py:641
  4.6 1.0 %copy-start.1 = (f32[32,32,128]{2,1,0:T(8,128)S(1)}, f32[32,32,128]{2,1,0:T(8,128)}, u32[]{:S(2)}) copy-start(f32[32,32,128]{2,1,0:T(8,128)} %f.3) | copy-start | bytes 1572868
  5.7 1.0 %copy-start.3 = (f32[32,32,128]{2,1,0:T(8,128)S(1)}, f32[32,32,128]{2,1,0:T(8,128)}, u32[]{:S(2)}) copy-start(f32[32,32,128]{2,1,0:T(8,128)} %k.1) | copy-start | bytes 1572868
  7.3 6.2 %collective-permute-start.1 = (f32[38,8,128]{2,1,0:T(8,128)S(1)}, f32[38,8,128]{2,1,0:T(8,128)S(1)}, u32[]{:S(2)}, u32[]{:S(2)}) collective-permute-start(f32[38,8,128]{2,1,0:T(8,128)S(1)} %get-tuple-element.51), channel_id=1, source_target_pairs={{0,16},{16,32},{32,48},{48,64},{64,80},{80,96},{96,112},{112,0},{1... | collective-permute-start | bytes 466952 | tf_op jit(solution)/shard_map/ppermute | solution.py:641
  10.2 4.7 %collective-permute-start.2 = (f32[38,8,128]{2,1,0:T(8,128)S(1)}, f32[38,8,128]{2,1,0:T(8,128)S(1)}, u32[]{:S(2)}, u32[]{:S(2)}) collective-permute-start(f32[38,8,128]{2,1,0:T(8,128)S(1)} %get-tuple-element.52), channel_id=1, source_target_pairs={{0,112},{16,0},{32,16},{48,32},{64,48},{80,64},{96,80},{112,96},{1... | collective-permute-start | bytes 466952 | tf_op jit(solution)/shard_map/ppermute | solution.py:641
  10.2 10.0 %collective-permute-start.10 = (f32[16,16,128]{2,1,0:T(8,128)S(1)}, f32[16,16,128]{2,1,0:T(8,128)S(1)}, u32[]{:S(2)}, u32[]{:S(2)}) collective-permute-start(f32[16,16,128]{2,1,0:T(8,128)S(1)} %get-tuple-element.70), channel_id=1, source_target_pairs={{0,1},{1,0},{2,3},{3,2},{4,5},{5,4},{6,7},{7,6},{8,9},{9,8},{10,11... | collective-permute-start | bytes 393224 | tf_op jit(solution)/shard_map/ppermute | solution.py:641
  15.2 8.9 %collective-permute-start.3 = (f32[3,40,128]{2,1,0:T(8,128)S(1)}, f32[3,40,128]{2,1,0:T(8,128)S(1)}, u32[]{:S(2)}, u32[]{:S(2)}) collective-permute-start(f32[3,40,128]{2,1,0:T(8,128)S(1)} %get-tuple-element.62), channel_id=1, source_target_pairs={{0,2},{2,4},{4,6},{6,8},{8,10},{10,12},{12,14},{14,0},{1,3},{3,5},... | collective-permute-start | bytes 184328 | tf_op jit(solution)/shard_map/ppermute | solution.py:641
  16.5 7.6 %collective-permute-start.4 = (f32[3,40,128]{2,1,0:T(8,128)S(1)}, f32[3,40,128]{2,1,0:T(8,128)S(1)}, u32[]{:S(2)}, u32[]{:S(2)}) collective-permute-start(f32[3,40,128]{2,1,0:T(8,128)S(1)} %get-tuple-element.63), channel_id=1, source_target_pairs={{0,14},{2,0},{4,2},{6,4},{8,6},{10,8},{12,10},{14,12},{1,15},{3,1}... | collective-permute-start | bytes 184328 | tf_op jit(solution)/shard_map/ppermute | solution.py:641
  20.2 3.9 %copy-start.2 = (f32[32,32,128]{2,1,0:T(8,128)S(1)}, f32[32,32,128]{2,1,0:T(8,128)}, u32[]{:S(2)}) copy-start(f32[32,32,128]{2,1,0:T(8,128)} %f.3) | copy-start | bytes 1572868
  20.5 7.6 %collective-permute-start.11 = (f32[7,16,128]{2,1,0:T(8,128)S(1)}, f32[7,16,128]{2,1,0:T(8,128)S(1)}, u32[]{:S(2)}, u32[]{:S(2)}) collective-permute-start(f32[7,16,128]{2,1,0:T(8,128)S(1)} %get-tuple-element.73), channel_id=1, source_target_pairs={{0,2},{2,4},{4,6},{6,8},{8,10},{10,12},{12,14},{14,0},{1,3},{3,5},... | collective-permute-start | bytes 172040 | tf_op jit(solution)/shard_map/ppermute | solution.py:641
  20.6 7.6 %collective-permute-start.12 = (f32[7,16,128]{2,1,0:T(8,128)S(1)}, f32[7,16,128]{2,1,0:T(8,128)S(1)}, u32[]{:S(2)}, u32[]{:S(2)}) collective-permute-start(f32[7,16,128]{2,1,0:T(8,128)S(1)} %get-tuple-element.74), channel_id=1, source_target_pairs={{0,14},{2,0},{4,2},{6,4},{8,6},{10,8},{12,10},{14,12},{1,15},{3,1}... | collective-permute-start | bytes 172040 | tf_op jit(solution)/shard_map/ppermute | solution.py:641
  25.6 4.7 %collective-permute-start.5 = (f32[8,16,128]{2,1,0:T(8,128)S(1)}, f32[8,16,128]{2,1,0:T(8,128)S(1)}, u32[]{:S(2)}, u32[]{:S(2)}) collective-permute-start(f32[8,16,128]{2,1,0:T(8,128)S(1)} %get-tuple-element.64), channel_id=1, source_target_pairs={{0,1},{1,0},{2,3},{3,2},{4,5},{5,4},{6,7},{7,6},{8,9},{9,8},{10,11... | collective-permute-start | bytes 196616 | tf_op jit(solution)/shard_map/ppermute | solution.py:641
  28.2 11.0 %collective-permute-start.14 = (f32[46,16,128]{2,1,0:T(8,128)S(1)}, f32[46,16,128]{2,1,0:T(8,128)S(1)}, u32[]{:S(2)}, u32[]{:S(2)}) collective-permute-start(f32[46,16,128]{2,1,0:T(8,128)S(1)} %pad_maximum_fusion.own), channel_id=1, source_target_pairs={{0,112},{16,0},{32,16},{48,32},{64,48},{80,64},{96,80},{112,96},{1... | collective-permute-start | bytes 1130504 | tf_op jit(solution)/shard_map/ppermute | solution.py:641
  29.3 9.8 %collective-permute-start.13 = (f32[46,16,128]{2,1,0:T(8,128)S(1)}, f32[46,16,128]{2,1,0:T(8,128)S(1)}, u32[]{:S(2)}, u32[]{:S(2)}) collective-permute-start(f32[46,16,128]{2,1,0:T(8,128)S(1)} %pad_maximum_fusion.own), channel_id=1, source_target_pairs={{0,16},{16,32},{32,48},{48,64},{64,80},{80,96},{96,112},{112,0},{1... | collective-permute-start | bytes 1130504 | tf_op jit(solution)/shard_map/ppermute | solution.py:641
  30.5 4.9 %collective-permute-start.6 = (f32[4,16,128]{2,1,0:T(8,128)S(1)}, f32[4,16,128]{2,1,0:T(8,128)S(1)}, u32[]{:S(2)}, u32[]{:S(2)}) collective-permute-start(f32[4,16,128]{2,1,0:T(8,128)S(1)} %get-tuple-element.66), channel_id=1, source_target_pairs={{0,2},{2,4},{4,6},{6,8},{8,10},{10,12},{12,14},{14,0},{1,3},{3,5},... | collective-permute-start | bytes 98312 | tf_op jit(solution)/shard_map/ppermute | solution.py:641
  30.5 4.9 %collective-permute-start.7 = (f32[4,16,128]{2,1,0:T(8,128)S(1)}, f32[4,16,128]{2,1,0:T(8,128)S(1)}, u32[]{:S(2)}, u32[]{:S(2)}) collective-permute-start(f32[4,16,128]{2,1,0:T(8,128)S(1)} %get-tuple-element.67), channel_id=1, source_target_pairs={{0,14},{2,0},{4,2},{6,4},{8,6},{10,8},{12,10},{14,12},{1,15},{3,1}... | collective-permute-start | bytes 98312 | tf_op jit(solution)/shard_map/ppermute | solution.py:641
  35.4 7.1 %collective-permute-start.9 = (f32[24,16,128]{2,1,0:T(8,128)S(1)}, f32[24,16,128]{2,1,0:T(8,128)S(1)}, u32[]{:S(2)}, u32[]{:S(2)}) collective-permute-start(f32[24,16,128]{2,1,0:T(8,128)S(1)} %constant_dynamic-update-slice_fusion.own), channel_id=1, source_target_pairs={{0,112},{16,0},{32,16},{48,32},{64,48},{80,64},{96,80},{112,96},{1... | collective-permute-start | bytes 589832 | tf_op jit(solution)/shard_map/ppermute | solution.py:641
  38.6 3.9 %collective-permute-start.8 = (f32[24,16,128]{2,1,0:T(8,128)S(1)}, f32[24,16,128]{2,1,0:T(8,128)S(1)}, u32[]{:S(2)}, u32[]{:S(2)}) collective-permute-start(f32[24,16,128]{2,1,0:T(8,128)S(1)} %constant_dynamic-update-slice_fusion.own), channel_id=1, source_target_pairs={{0,16},{16,32},{32,48},{48,64},{64,80},{80,96},{96,112},{112,0},{1... | collective-permute-start | bytes 589832 | tf_op jit(solution)/shard_map/ppermute | solution.py:641
